TPU v7x, 128 devices: a whole 4x4x4 slice. The times are simulated.
128 devices in a mesh: cache: 8 (over z, core), head: 16 (over x, y).
Axes of the slice: x: 4, y: 4, z: 4, core: 2. Of those that a mesh axis runs over, the one named last changes fastest.
Arguments:
- delta_query: bfloat16 [32, 512, 2048], P('cache', None, 'head'), may hold values from -6 to 6
- delta_key: bfloat16 [32, 512, 2048], P('cache', None, 'head'), may hold values from -6 to 6
- delta_value: bfloat16 [32, 512, 4096], P('cache', None, 'head'), may hold values from -6 to 6
- delta_gate: bfloat16 [32, 512, 4096], P('cache', None, 'head'), may hold values from -6 to 6
- write_strength: float32 [32, 32, 512], P('cache', 'head'), may hold values from 0.1 to 0.95
- decay_log: float32 [32, 32, 512], P('cache', 'head'), may hold values from -1.5 to 0
- kept_state: float32 [32, 32, 128, 128], P('cache', 'head'), may hold values from -6 to 6
- kept_kv: bfloat16 [32, 1024, 2, 512], P('cache', 'head'), may hold values from -8 to 8
- fresh_kv: bfloat16 [32, 512, 2, 512], P('cache', 'head'), may hold values from -6 to 6
- attn_query: bfloat16 [32, 512, 4096], P('cache', None, 'head'), may hold values from -100 to 100
- attn_gate: bfloat16 [32, 512, 4096], P('cache', None, 'head'), may hold values from -6 to 6
- cached_len: int32 [32], replicated, may hold values from 2 to 1024, as said below
- slot_of_session: int32 [32], replicated, may hold values from 0 to 31, as said below
- delta_out_weight: bfloat16 [4096, 2048], P('head'), may hold values from -0.09375 to 0.09375
- attn_out_weight: bfloat16 [4096, 2048], P('head'), may hold values from -0.75 to 0.75
Outputs:
- delta_mixed: bfloat16 [16384, 2048], P(('cache', 'head'))
- attn_mixed: bfloat16 [16384, 2048], P(('cache', 'head'))
- final_state: float32 [32, 32, 128, 128], P('cache', 'head')
Inputs may be any that keep to these rules, and one draw needn't show every extreme that they name: `slot_of_session`: a permutation of the slots; slot r lies on cache shard floor(r / 4); session s belongs to owner floor(s / 4), and the 4 sessions of one owner are kept on 4 different shards. `cached_len`: some session keeps exactly 1024 positions.
All inputs are finite; a program needn't handle non-finite values.
Results may differ from a plain program's by a relative error of at most 0.02.
Values may be sent and summed in bfloat16 or wider, within the bound.
No kernel may reach another device: no remote copies, remote signals or barrier semaphores. Data moves between devices by JAX's collectives and lax.ppermute only.
A program may use at most 128 MiB of HBM per device.

v0:
```python
import math

import jax
import jax.numpy as jnp
from jax import lax
from jax.sharding import PartitionSpec as P

LK = 128
LV = 128
AH = 16
KVH = 2
HD = 256


big_negative = -1e30
highest = lax.Precision.HIGHEST


def unit_rows(matrix, epsilon):
    return matrix / jnp.sqrt(jnp.sum(matrix * matrix, axis=-1, keepdims=True) + epsilon)


def recurrent_segments(
    delta_query, delta_key, delta_value, delta_gate, write_strength, decay_log, state_start
):
    count, fresh_len, key_cols = delta_query.shape
    key_heads = key_cols // LK
    value_heads = delta_value.shape[2] // LV
    block_len = 64
    blocks = fresh_len // block_len
    share_ratio = value_heads // key_heads
    query_matrix = unit_rows(
        delta_query.astype(jnp.float32).reshape(count, fresh_len, key_heads, LK), 1e-06
    ) * (1.0 / math.sqrt(LK))
    keyed = unit_rows(delta_key.astype(jnp.float32).reshape(count, fresh_len, key_heads, LK), 1e-06)
    query_matrix = jnp.repeat(query_matrix, share_ratio, axis=2)
    keyed = jnp.repeat(keyed, share_ratio, axis=2)
    values = delta_value.astype(jnp.float32).reshape(count, fresh_len, value_heads, LV)

    def arrange(matrix):
        return matrix.reshape(count, blocks, block_len, value_heads, matrix.shape[-1]).transpose(
            1, 0, 3, 2, 4
        )

    def arrange_rates(rates):
        return rates.reshape(count, value_heads, blocks, block_len).transpose(2, 0, 1, 3)

    offsets = jnp.arange(block_len)
    strict = offsets[:, None] > offsets[None, :]
    inclusive = offsets[:, None] >= offsets[None, :]
    identity_block = jnp.eye(block_len, dtype=jnp.float32)

    def advance(carried, pieces):
        q_blk, k_blk, v_blk, b_blk, g_blk = pieces
        running = jnp.cumsum(g_blk, axis=-1)
        between = running[..., :, None] - running[..., None, :]
        fall_strict = jnp.where(strict, jnp.exp(jnp.where(strict, between, 0.0)), 0.0)
        fall_upto = jnp.where(inclusive, jnp.exp(jnp.where(inclusive, between, 0.0)), 0.0)
        key_key = jnp.einsum("shtk,shuk->shtu", k_blk, k_blk, precision=highest)
        negated = -(b_blk[..., :, None] * fall_strict * key_key)
        inverse = identity_block + negated
        power = negated
        for level in range(block_len.bit_length() - 1):
            power = jnp.matmul(power, power, precision=highest)
            inverse = jnp.matmul(inverse, identity_block + power, precision=highest)
        growth = jnp.exp(running)[..., None]
        right_side = jnp.concatenate(
            [b_blk[..., None] * growth * k_blk, b_blk[..., None] * v_blk], axis=-1
        )
        solved = jnp.matmul(inverse, right_side, precision=highest)
        update = solved[..., LK:] - jnp.einsum(
            "shtk,shkv->shtv", solved[..., :LK], carried, precision=highest
        )
        query_key = jnp.einsum("shtk,shuk->shtu", q_blk, k_blk, precision=highest)
        emitted = growth * jnp.einsum("shtk,shkv->shtv", q_blk, carried, precision=highest)
        emitted = emitted + jnp.einsum(
            "shtu,shuv->shtv", fall_upto * query_key, update, precision=highest
        )
        tail_fade = jnp.exp(running[..., -1:] - running)[..., None]
        carried = jnp.exp(running[..., -1])[..., None, None] * carried
        carried = carried + jnp.einsum(
            "shtk,shtv->shkv", tail_fade * k_blk, update, precision=highest
        )
        return (carried, emitted)

    final_state, emitted = lax.scan(
        advance,
        state_start,
        (
            arrange(query_matrix),
            arrange(keyed),
            arrange(values),
            arrange_rates(write_strength),
            arrange_rates(decay_log),
        ),
    )
    emitted = emitted.transpose(1, 0, 3, 2, 4).reshape(count, fresh_len, value_heads, LV)
    normed = emitted / jnp.sqrt(jnp.mean(emitted * emitted, axis=-1, keepdims=True) + 1e-06)
    gate_f = delta_gate.astype(jnp.float32).reshape(count, fresh_len, value_heads, LV)
    heads = (
        (normed * jax.nn.silu(gate_f))
        .astype(jnp.bfloat16)
        .reshape(count * fresh_len, value_heads * LV)
    )
    return (heads, final_state)


def on_device(
    delta_query,
    delta_key,
    delta_value,
    delta_gate,
    write_strength,
    decay_log,
    kept_state,
    kept_kv,
    fresh_kv,
    attn_query,
    attn_gate,
    cached_len,
    slot_of_session,
    delta_out_weight,
    attn_out_weight,
):
    count, fresh_len, query_cols = attn_query.shape
    owners = lax.axis_size("cache")
    owner_id = lax.axis_index("cache")
    session_ids = jnp.arange(slot_of_session.shape[0], dtype=jnp.int32)
    on_mine = slot_of_session // count == owner_id
    owner_of = session_ids // count
    wanted = on_mine[None, :] & (owner_of[None, :] == jnp.arange(owners, dtype=jnp.int32)[:, None])
    picked_slot = jnp.sum(jnp.where(wanted, slot_of_session[None, :] - owner_id * count, 0), axis=1)
    my_slots = lax.dynamic_slice_in_dim(slot_of_session, owner_id * count, count)
    source = my_slots // count
    lengths = lax.dynamic_slice_in_dim(cached_len, owner_id * count, count)
    arrived = lax.all_to_all(
        jnp.take(kept_state, picked_slot, axis=0).astype(jnp.bfloat16),
        "cache",
        split_axis=0,
        concat_axis=0,
        tiled=True,
    ).astype(jnp.float32)
    state_start = jnp.take(arrived, source, axis=0)
    landed = lax.all_to_all(
        jnp.take(kept_kv, picked_slot, axis=0), "cache", split_axis=0, concat_axis=0, tiled=True
    )
    cache_block = jnp.take(landed, source, axis=0)
    delta_heads, final_state = recurrent_segments(
        delta_query, delta_key, delta_value, delta_gate, write_strength, decay_log, state_start
    )
    taken = delta_heads
    delta_mixed = lax.psum_scatter(
        jnp.dot(taken, delta_out_weight, preferred_element_type=jnp.float32).astype(jnp.bfloat16),
        "head",
        scatter_dimension=0,
        tiled=True,
    )
    score_scale = 1.0 / math.sqrt(HD)
    heads_dev = query_cols // HD
    kv_group = AH // KVH
    head_id = lax.axis_index("head")
    kv_head = head_id * heads_dev // kv_group
    query_matrix = attn_query.reshape(count, fresh_len, heads_dev, HD).transpose(0, 2, 1, 3)

    def absorb(partial_value, key_row_matrix, value_rows, usable):
        peak_now, total_w, weighted = partial_value
        scores = (
            jnp.einsum(
                "mrci,mji->mrcj", query_matrix, key_row_matrix, preferred_element_type=jnp.float32
            )
            * score_scale
        )
        usable_four = usable[:, None]
        masked = jnp.where(usable_four, scores, big_negative)
        peak_new = jnp.maximum(peak_now, jnp.max(masked, axis=-1))
        weights = jnp.where(usable_four, jnp.exp(masked - peak_new[..., None]), 0.0)
        fade_old = jnp.exp(peak_now - peak_new)
        total_w = total_w * fade_old + jnp.sum(weights, axis=-1)
        weighted = weighted * fade_old[..., None] + jnp.einsum(
            "guqx,gxp->guqp",
            weights.astype(jnp.bfloat16),
            value_rows,
            preferred_element_type=jnp.float32,
        )
        return (peak_new, total_w, weighted)

    steps_new = jnp.arange(fresh_len, dtype=jnp.int32)
    causal = (steps_new[None, :] <= steps_new[:, None])[None]
    start_partial = (
        jnp.full((count, heads_dev, fresh_len), big_negative, jnp.float32),
        jnp.zeros((count, heads_dev, fresh_len), jnp.float32),
        jnp.zeros((count, heads_dev, fresh_len, HD), jnp.float32),
    )
    fresh_all = lax.all_gather(fresh_kv, "head", axis=1, tiled=True)
    chosen = lax.dynamic_slice_in_dim(fresh_all, kv_head * HD, HD, 3)
    partial_value = absorb(start_partial, chosen[:, :, 0], chosen[:, :, 1], causal)
    piece_rows = lax.all_gather(cache_block, "head", axis=1, tiled=True)
    taken = lax.dynamic_slice_in_dim(piece_rows, kv_head * HD, HD, 3)
    sequence_offset = jnp.arange(piece_rows.shape[1], dtype=jnp.int32)
    partial_value = absorb(
        partial_value,
        taken[:, :, 0],
        taken[:, :, 1],
        sequence_offset[None, None, :] < lengths[:, None, None],
    )
    mixed = (partial_value[2] / partial_value[1][..., None]).transpose(0, 2, 1, 3)
    gate_f = attn_gate.astype(jnp.float32).reshape(count, fresh_len, heads_dev, HD)
    attn_heads = (
        (jax.nn.sigmoid(gate_f) * mixed)
        .astype(jnp.bfloat16)
        .reshape(count * fresh_len, heads_dev * HD)
    )
    taken = attn_heads
    attn_mixed = lax.psum_scatter(
        jnp.dot(taken, attn_out_weight, preferred_element_type=jnp.float32).astype(jnp.bfloat16),
        "head",
        scatter_dimension=0,
        tiled=True,
    )
    return (delta_mixed, attn_mixed, final_state)


def solution(mesh):
    in_specs = (
        P("cache", None, "head"),
        P("cache", None, "head"),
        P("cache", None, "head"),
        P("cache", None, "head"),
        P("cache", "head", None),
        P("cache", "head", None),
        P("cache", "head", None, None),
        P("cache", "head", None, None),
        P("cache", "head", None, None),
        P("cache", None, "head"),
        P("cache", None, "head"),
        P(),
        P(),
        P("head", None),
        P("head", None),
    )
    out_specs = (
        P(("cache", "head"), None),
        P(("cache", "head"), None),
        P("cache", "head", None, None),
    )
    return jax.shard_map(
        on_device, mesh=mesh, in_specs=in_specs, out_specs=out_specs, check_vma=False
    )
```

profile of v0, /device:TPU:0, one launch (start us, length us, event | category | flops | bytes accessed | tf_op | source)
XLA Modules:
  0.0 388.4 jit_solution(9163193233267216933)
XLA Ops:
  13.3 5.4 %all-to-all-start = ((bf16[8,2,128,128]{3,2,1,0:T(8,128)(2,1)}), bf16[8,2,128,128]{3,2,1,0:T(8,128)(2,1)}, u32[]{:S(2)}, u32[]{:S(2)}) async-start(bf16[8,2,128,128]{3,2,1,0:T(8,128)(2,1)} %select_convert_fusion), calls=%async_computation | async-start | bytes 1048576 | tf_op jit(solution)/shard_map/all_to_all | solution.py:136
  20.9 2.7 gather_fusion.2
  25.6 3.6 all-to-all-done
  29.2 3.6 all-to-all-start.1
  32.8 3.1 reshape.298
  36.4 3.5 broadcast_bitcast_fusion
  39.9 2.2 convert_element_type.55
  44.0 4.6 %all-to-all-done.1 = bf16[8,64,2,512]{3,2,1,0:T(2,128)(2,1)S(1)} async-done(((bf16[8,64,2,512]{3,2,1,0:T(2,128)(2,1)}), bf16[8,64,2,512]{3,2,1,0:T(2,128)(2,1)S(1)}, u32[]{:S(2)}, u32[]{:S(2)}) %all-to-all-start.1) | async-done | bytes 1048608 | tf_op jit(solution)/shard_map/all_to_all | solution.py:144
  52.8 141.1 %while.14 = (s32[]{:T(128)}, f32[4,2,128,128]{3,2,1,0:T(8,128)S(1)}, f32[8,4,2,64,128]{4,3,2,1,0:T(8,128)}, f32[8,4,2,64]{3,0,2,1:T(8,128)S(1)}, f32[8,4,2,64,12...) while((s32[]{:T(128)}, ...), condition=%wide.region_5.6_spmd.clone.clone, body=%wide.region_3.5_spmd.clone.clone.sunk | while | flops 857031168 | bytes 12776949 | solution.py:86
  68.2 2.2 convolution_add_fusion.6
  85.9 2.2 convolution_add_fusion.6
  121.3 2.2 convolution_add_fusion.6
  193.9 2.4 multiply_reduce_fusion
  196.8 3.4 copy.107
  200.2 2.8 div.104
  203.0 5.9 %convolution_convert_fusion.1 = bf16[2048,2048]{1,0:T(8,128)(2,1)} fusion(bf16[256,2048]{1,0:T(8,128)(2,1)S(1)} %copy-done, bf16[2048,256]{1,0:T(8,128)(2,1)S(1)} %bitcast.223, f32[256,8,2,128]{3,2,1,0:T(2,128)S(1)} %bitcast.213, f32[256,8,2,128]{3,2,1,0:T(2,128)S(1)} %bitcast.214), kind=kOutput, calls=%fused_computation.80 | convolution fusion | flops 2155872256 | bytes 14680064 | tf_op jit(solution)/shard_map/dot_general | solution.py:153
  210.2 4.1 %fusion.60 = (f32[4,512]{1,0:T(4,128)S(1)}, f32[4,512,512]{2,1,0:T(8,128)}) fusion(pred[512,512]{0,1:T(8,128)(4,1)S(1)} %iota_compare_fusion.3, bf16[4,512,256]{2,1,0:T(8,128)(2,1)S(1)} %copy-done.12, bf16[4,512,2,512]{3,1,0,2:T(8,128)(2,1)} %all-gather.3.cloned.1.call-done, s32[]{:T(128)S(6)} %select_n.119), kind=kOutput, calls=%fused_computation.88 | convolution fusion | flops 540014592 | bytes 6561796 | tf_op jit(solution)/shard_map/mrci,mji->mrcj/dot_general | solution.py:168
  214.2 3.8 bitcast_reduce_fusion
  219.1 2.8 fusion.54
  222.0 2.9 fusion.67
  224.9 5.9 %multiply_convert_fusion = bf16[4,512,256]{2,1,0:T(8,128)(2,1)S(1)} fusion(f32[4,512,256]{2,1,0:T(8,128)S(1)} %fusion.67, bf16[4,512,256]{2,1,0:T(8,128)(2,1)S(1)} %copy-done.13, bf16[4,1024,2,512]{3,1,0,2:T(8,128)(2,1)} %all-gather.5.cloned.1.call-done, s32[]{:T(128)S(6)} %add.214, s32[]{:T(128)S(6)} %select_n.119, ...), kind=kOutput, calls=%fused_computation.102 | convolution fusion | flops 1089470464 | bytes 14721032 | tf_op jit(solution)/shard_map/guqx,gxp->guqp/dot_general | solution.py:179
  230.8 5.6 %convolution_convert_fusion = bf16[2048,2048]{1,0:T(8,128)(2,1)} fusion(bf16[2048,256]{1,0:T(8,128)(2,1)S(1)} %bitcast.215, bf16[256,2048]{1,0:T(8,128)(2,1)S(1)} %copy-done.7), kind=kOutput, calls=%fused_computation.79 | convolution fusion | flops 2151677952 | bytes 10485760 | tf_op jit(solution)/shard_map/dot_general | solution.py:215
  236.4 57.2 %reduce-scatter.3.cloned.1.call-done = bf16[128,2048]{1,0:T(8,128)(2,1)} async-done(((bf16[2048,2048]{1,0:T(8,128)(2,1)}), bf16[128,2048]{1,0:T(8,128)(2,1)}) %reduce-scatter.3.cloned.1.call-update) | async-done | bytes 524304 | tf_op jit(solution)/shard_map/reduce_scatter | solution.py:152
  293.6 88.2 %reduce-scatter.5.cloned.1.call-done = bf16[128,2048]{1,0:T(8,128)(2,1)} async-done(((bf16[2048,2048]{1,0:T(8,128)(2,1)}), bf16[128,2048]{1,0:T(8,128)(2,1)}) %reduce-scatter.5.cloned.1.call-update) | async-done | bytes 524304 | tf_op jit(solution)/shard_map/reduce_scatter | solution.py:214
  (335 shorter events, 152.8 us)
Async XLA Ops:
  7.2 195.8 %copy-start = (bf16[256,2048]{1,0:T(8,128)(2,1)S(1)}, bf16[256,2048]{1,0:T(8,128)(2,1)}, u32[]{:S(2)}) copy-start(bf16[256,2048]{1,0:T(8,128)(2,1)} %param.30) | copy-start | bytes 3145732
  7.2 11.5 %copy-start.4 = (bf16[4,512,128]{2,1,0:T(8,128)(2,1)S(1)}, bf16[4,512,128]{2,1,0:T(8,128)(2,1)}, u32[]{:S(2)}) copy-start(bf16[4,512,128]{2,1,0:T(8,128)(2,1)} %param.18) | copy-start | bytes 1572868
  7.2 11.9 %copy-start.6 = (bf16[4,512,128]{2,1,0:T(8,128)(2,1)S(1)}, bf16[4,512,128]{2,1,0:T(8,128)(2,1)}, u32[]{:S(2)}) copy-start(bf16[4,512,128]{2,1,0:T(8,128)(2,1)} %param.17) | copy-start | bytes 1572868
  7.2 13.6 %copy-start.5 = (bf16[4,64,2,512]{3,2,1,0:T(2,128)(2,1)S(1)}, bf16[4,64,2,512]{3,2,1,0:T(2,128)(2,1)}, u32[]{:S(2)}) copy-start(bf16[4,64,2,512]{3,2,1,0:T(2,128)(2,1)} %param.24) | copy-start | bytes 1572868
  7.2 202.6 %all-gather.3.cloned.1.call-start = ((), (), s32[]{:S(2)}) async-start(), calls=%async_computation.5 | async-start | bytes 4456448 | tf_op jit(solution)/shard_map/all_gather | solution.py:194
  9.1 14.5 %copy-start.10 = (s32[32]{0:T(128)S(1)}, s32[32]{0:T(128)}, u32[]{:S(2)}) copy-start(s32[32]{0:T(128)} %param.29) | copy-start | bytes 388
  13.3 15.9 %all-to-all-start = ((bf16[8,2,128,128]{3,2,1,0:T(8,128)(2,1)}), bf16[8,2,128,128]{3,2,1,0:T(8,128)(2,1)}, u32[]{:S(2)}, u32[]{:S(2)}) async-start(bf16[8,2,128,128]{3,2,1,0:T(8,128)(2,1)} %select_convert_fusion), calls=%async_computation | async-start | bytes 1048576 | tf_op jit(solution)/shard_map/all_to_all | solution.py:136
  23.5 12.4 %copy-start.8 = (f32[4,2,512]{2,1,0:T(2,128)S(1)}, f32[4,2,512]{2,1,0:T(2,128)}, u32[]{:S(2)}) copy-start(f32[4,2,512]{2,1,0:T(2,128)} %param.22) | copy-start | bytes 49156
  23.5 12.5 %copy-start.9 = (f32[4,2,512]{2,1,0:T(2,128)S(1)}, f32[4,2,512]{2,1,0:T(2,128)}, u32[]{:S(2)}) copy-start(f32[4,2,512]{2,1,0:T(2,128)} %param.21) | copy-start | bytes 49156
  29.2 19.4 %all-to-all-start.1 = ((bf16[8,64,2,512]{3,2,1,0:T(2,128)(2,1)}), bf16[8,64,2,512]{3,2,1,0:T(2,128)(2,1)S(1)}, u32[]{:S(2)}, u32[]{:S(2)}) async-start(bf16[8,64,2,512]{3,2,1,0:T(2,128)(2,1)} %broadcast_select_fusion), calls=%async_computation.2 | async-start | bytes 2097152 | tf_op jit(solution)/shard_map/all_to_all | solution.py:144
  32.7 181.5 %all-gather.5.cloned.1.call-start = ((), (), s32[]{:S(2)}) async-start(), calls=%async_computation.6 | async-start | bytes 8912896 | tf_op jit(solution)/shard_map/all_gather | solution.py:197
  52.5 241.1 %reduce-scatter.3.cloned.1.call-start = ((), (), s32[]{:S(2)}) async-start(), calls=%async_computation.4 | async-start | bytes 8912896 | tf_op jit(solution)/shard_map/reduce_scatter | solution.py:152
  193.9 9.0 %copy-start.2 = (f32[4,2,128,128]{3,2,1,0:T(8,128)}, f32[4,2,128,128]{3,2,1,0:T(8,128)S(1)}, u32[]{:S(2)}) copy-start(f32[4,2,128,128]{3,2,1,0:T(8,128)S(1)} %get-tuple-element.84) | copy-start | bytes 1572868
  196.8 6.2 %copy-start.11 = (bf16[4,512,256]{2,1,0:T(8,128)(2,1)S(1)}, bf16[4,512,256]{2,1,0:T(8,128)(2,1)}, u32[]{:S(2)}) copy-start(bf16[4,512,256]{2,1,0:T(8,128)(2,1)} %param.20) | copy-start | bytes 3145732
  208.9 0.7 copy-start.14
  208.9 1.2 copy-start.12
  208.9 172.9 %reduce-scatter.5.cloned.1.call-start = ((), (), s32[]{:S(2)}) async-start(), calls=%async_computation.7 | async-start | bytes 8912896 | tf_op jit(solution)/shard_map/reduce_scatter | solution.py:214
  214.2 3.8 copy-start.3
  222.0 2.9 copy-start.13
  224.8 5.9 %copy-start.7 = (bf16[256,2048]{1,0:T(8,128)(2,1)S(1)}, bf16[256,2048]{1,0:T(8,128)(2,1)}, u32[]{:S(2)}) copy-start(bf16[256,2048]{1,0:T(8,128)(2,1)} %param.31) | copy-start | bytes 3145732
  236.4 145.5 %copy-start.1 = (bf16[256,2048]{1,0:T(8,128)(2,1)S(1)}, bf16[256,2048]{1,0:T(8,128)(2,1)}, u32[]{:S(2)}) copy-start(bf16[256,2048]{1,0:T(8,128)(2,1)} %param.30) | copy-start | bytes 3145732
Sparse Core Ops, SparseCore 0:
  10.2 53.9 all-gather.2
  67.0 70.4 all-gather.4
  209.1 84.5 reduce-scatter.2
  297.5 84.3 reduce-scatter.4
where the time goes:
time: 390 us; the launch traced here: 388 us
  waiting for transfers between devices  154 us (39%)
  matrix products  139 us (36%)
  local copies, waits for them, and re-layouts  36.1 us (9%)
  other arithmetic  35 us (9%)
  between operations  14.1 us (4%)
  starting transfers between devices  9.3 us (2%)
    reduce_scatter x1, waiting for transfers between devices, on_device(): lax.psum_scatter(jnp.dot(taken, attn_out_weight, preferred_element_type=j...  88.2 us
    reduce_scatter x1, waiting for transfers between devices, on_device(): lax.psum_scatter(jnp.dot(taken, delta_out_weight, preferred_element_type=...  57.2 us
    dot_general x48, matrix products, advance(): inverse = jnp.matmul(inverse, identity_block + power, precision=highest)  18.7 us
    dot_general x48, matrix products, advance(): power = jnp.matmul(power, power, precision=highest)  18.4 us
    dot_general x8, matrix products, advance(): jnp.einsum('shtk,shtv->shkv', tail_fade * k_blk, update, precision=highest)  17.3 us
    dot_general x8, matrix products, advance(): query_key = jnp.einsum('shtk,shuk->shtu', q_blk, k_blk, precision=highest)  12.7 us
    dot_general x8, matrix products, advance(): key_key = jnp.einsum('shtk,shuk->shtu', k_blk, k_blk, precision=highest)  12.7 us
    dot_general x8, matrix products, advance(): jnp.einsum('shtk,shkv->shtv', q_blk, carried, precision=highest)  12.4 us
  transfers between devices with their start and end apart: 6, of which 4 were waited for; matrix products, arithmetic and copies ran while one was open for 53% of the time, Pallas kernels for 0%

commit v1 on v0

v1 whole, which is shorter than its diff:
```python
import functools
import math

import jax
import jax.numpy as jnp
import numpy as np
from jax import lax
from jax.experimental import pallas as pl
from jax.experimental.pallas import tpu as pltpu
from jax.sharding import Mesh, PartitionSpec as P

F32 = jnp.float32
BF16 = jnp.bfloat16
CH = 128
HIGH = lax.Precision.HIGHEST
NEG = -1e30
VMEM = 60 * 1024 * 1024


def cost(us):
    return pl.CostEstimate(flops=int(us * 1e9), transcendentals=0, bytes_accessed=int(us * 3e6))


def after(value, *others):
    return lax.optimization_barrier((value, others))[0]


def mm(a, b):
    return lax.dot_general(a, b, (((1,), (0,)), ((), ())), preferred_element_type=F32)


def mm_nt(a, b, precision=None):
    return lax.dot_general(
        a, b, (((1,), (1,)), ((), ())), preferred_element_type=F32, precision=precision
    )


def prep_kernel(q_ref, k_ref, v_ref, b_ref, g_ref, wq_ref, u_ref, p_ref, kt_ref, dec_ref):
    row = lax.broadcasted_iota(jnp.int32, (CH, CH), 0)
    col = lax.broadcasted_iota(jnp.int32, (CH, CH), 1)
    strict = row > col
    incl = row >= col
    diag = row == col
    tri = jnp.where(incl, 1.0, 0.0).astype(F32)
    eye = jnp.where(diag, 1.0, 0.0).astype(F32)
    g8 = jnp.concatenate([g_ref[s] for s in range(4)], axis=0)
    b8 = jnp.concatenate([b_ref[s] for s in range(4)], axis=0)
    g_rows = mm_nt(g8, tri, HIGH)
    g_cols = mm_nt(tri, g8, HIGH)
    b_cols = mm_nt(eye, b8, HIGH)
    chains = []
    for s in range(4):
        k = k_ref[s]
        q = q_ref[s]
        kk = mm_nt(k, k)
        qk = mm_nt(q, k)
        kf = k.astype(F32)
        qf = q.astype(F32)
        rk = lax.rsqrt(jnp.sum(kf * kf, axis=1, keepdims=True) + 1e-6)
        rq = lax.rsqrt(jnp.sum(qf * qf, axis=1, keepdims=True) + 1e-6) * (1.0 / math.sqrt(128.0))
        rk_row = lax.rsqrt(jnp.sum(jnp.where(diag, kk, 0.0), axis=0, keepdims=True) + 1e-6)
        kkn = kk * rk * rk_row
        qkn = qk * rq * rk_row
        kn = kf * rk
        qn = qf * rq
        for h in range(2):
            i = 2 * s + h
            gc = g_cols[:, i : i + 1]
            gr = g_rows[i : i + 1, :]
            bc = b_cols[:, i : i + 1]
            decay = jnp.where(incl, jnp.exp(jnp.where(incl, gc - gr, 0.0)), 0.0)
            low = jnp.where(strict, decay * kkn * bc, 0.0)
            p_ref[0, i] = (decay * qkn).astype(BF16)
            growth = jnp.exp(gc)
            g_last = gr[:, CH - 1 : CH]
            tail = jnp.exp(g_last - gc)
            kt_ref[0, i] = (tail * kn).T.astype(BF16)
            wq_ref[0, i, CH:, :] = (growth * qn).astype(BF16)
            dec_ref[0, i : i + 1, :] = jnp.broadcast_to(jnp.exp(g_last), (1, CH))
            rhs = jnp.concatenate(
                [bc * v_ref[s, :, h * CH : (h + 1) * CH].astype(F32), (bc * growth) * kn], axis=1
            ).astype(BF16)
            chains.append([low, rhs])
    inverses = []
    pair = (row // 2 == col // 2) & strict
    for low, _ in chains:
        inverses.append(eye - jnp.where(pair, low, 0.0))
    m = 2
    while m < CH:
        mask = (row // (2 * m) == col // (2 * m)) & (row // m > col // m)
        lefts = [
            mm(jnp.where(mask, chains[i][0], 0.0).astype(BF16), inverses[i].astype(BF16))
            for i in range(8)
        ]
        steps = [mm(inverses[i].astype(BF16), lefts[i].astype(BF16)) for i in range(8)]
        inverses = [inverses[i] - steps[i] for i in range(8)]
        m *= 2
    for i in range(8):
        solved = mm(inverses[i].astype(BF16), chains[i][1])
        u_ref[0, i] = solved[:, :CH]
        wq_ref[0, i, :CH, :] = solved[:, CH:].astype(BF16)


def prep(delta_query, delta_key, delta_value, strengths, decays):
    chunks = delta_query.shape[1] // CH
    spec_tok = lambda w: pl.BlockSpec((4, CH, w), lambda c: (0, c, 0))
    spec_rate = pl.BlockSpec((4, 2, CH), lambda c: (0, 0, c))
    spec_out = lambda r: pl.BlockSpec((1, 8, r, CH), lambda c: (c, 0, 0, 0))
    shape = lambda r, t: jax.ShapeDtypeStruct((chunks, 8, r, CH), t)
    return pl.pallas_call(
        prep_kernel,
        grid=(chunks,),
        in_specs=[spec_tok(CH), spec_tok(CH), spec_tok(2 * CH), spec_rate, spec_rate],
        out_specs=[
            spec_out(2 * CH),
            spec_out(CH),
            spec_out(CH),
            spec_out(CH),
            pl.BlockSpec((1, 8, CH), lambda c: (c, 0, 0)),
        ],
        out_shape=[
            shape(2 * CH, BF16),
            shape(CH, F32),
            shape(CH, BF16),
            shape(CH, BF16),
            jax.ShapeDtypeStruct((chunks, 8, CH), F32),
        ],
        compiler_params=pltpu.CompilerParams(vmem_limit_bytes=VMEM),
        cost_estimate=cost(0.1),
        name="delta_prep",
    )(delta_query, delta_key, delta_value, strengths, decays)


def scan_kernel(
    src_ref, state_ref, wq_ref, u_ref, p_ref, kt_ref, dec_ref, gate_ref, heads_ref, final_ref, carry
):
    c = pl.program_id(0)

    @pl.when(c == 0)
    def _():
        for s in range(4):
            for h in range(2):
                for j in range(4):
                    block = state_ref[src_ref[s], 32 * h : 32 * h + 32, j * CH : (j + 1) * CH]
                    carry[2 * s + h, 32 * j : 32 * j + 32, :] = block.astype(F32)

    states = [carry[i] for i in range(8)]
    reads = [mm(wq_ref[0, i], states[i].astype(BF16)) for i in range(8)]
    updates = [(u_ref[0, i] - reads[i][:CH]).astype(BF16) for i in range(8)]
    for i in range(8):
        carry[i] = states[i] * dec_ref[0, i : i + 1, :] + mm(kt_ref[0, i], updates[i])
    for i in range(8):
        s, h = i // 2, i % 2
        out = reads[i][CH:] + mm(p_ref[0, i], updates[i])
        scale = lax.rsqrt(jnp.mean(out * out, axis=1, keepdims=True) + 1e-6)
        gate = gate_ref[s, :, h * CH : (h + 1) * CH].astype(F32)
        silu = gate / (1.0 + jnp.exp(-gate))
        heads_ref[0, s, :, h * CH : (h + 1) * CH] = (out * scale * silu).astype(BF16)

    @pl.when(c == pl.num_programs(0) - 1)
    def _():
        for s in range(4):
            for h in range(2):
                final_ref[s, h] = carry[2 * s + h]


def scan(source, arrived, prepared, delta_gate):
    wq, u0, p, kt, dec = prepared
    chunks = wq.shape[0]
    spec = lambda r: pl.BlockSpec((1, 8, r, CH), lambda c, *_: (c, 0, 0, 0))
    return pl.pallas_call(
        scan_kernel,
        grid_spec=pltpu.PrefetchScalarGridSpec(
            num_scalar_prefetch=1,
            grid=(chunks,),
            in_specs=[
                pl.BlockSpec((8, 64, 512), lambda c, *_: (0, 2, 0)),
                spec(2 * CH),
                spec(CH),
                spec(CH),
                spec(CH),
                pl.BlockSpec((1, 8, CH), lambda c, *_: (c, 0, 0)),
                pl.BlockSpec((4, CH, 2 * CH), lambda c, *_: (0, c, 0)),
            ],
            out_specs=[
                pl.BlockSpec((1, 4, CH, 2 * CH), lambda c, *_: (c, 0, 0, 0)),
                pl.BlockSpec((4, 2, CH, CH), lambda c, *_: (0, 0, 0, 0)),
            ],
            scratch_shapes=[pltpu.VMEM((8, CH, CH), F32)],
        ),
        out_shape=[
            jax.ShapeDtypeStruct((chunks, 4, CH, 2 * CH), BF16),
            jax.ShapeDtypeStruct((4, 2, CH, CH), F32),
        ],
        compiler_params=pltpu.CompilerParams(vmem_limit_bytes=VMEM),
        cost_estimate=cost(0.1),
        name="delta_scan",
    )(source, arrived, wq, u0, p, kt, dec, delta_gate)


def swap_halves(core, head):
    low, high = head[:, :CH], head[:, CH:]
    return jnp.concatenate(
        [jnp.where(core == 0, low, high), jnp.where(core == 0, high, low)], axis=1
    )


def delta_project_kernel(sc_ref, heads_ref, own_ref, other_ref, *outs):
    x, y, core = sc_ref[0], sc_ref[1], sc_ref[2]
    total = None
    for e in range(4):
        rows = jnp.concatenate([heads_ref[(y - e) & 3, (x + d) & 3] for d in range(4)], axis=0)
        weight = jnp.concatenate([own_ref[e], other_ref[e]], axis=0)
        part = mm(swap_halves(core, rows), weight)
        total = part if total is None else total + part
    total = total.astype(BF16)
    for d, ref in enumerate(outs):
        ref[...] = total[d * CH : (d + 1) * CH]


def delta_project(scalars, pieces, own, other):
    weight = pl.BlockSpec((4, CH, 512), lambda i, sc: (0, i, 0))
    return pl.pallas_call(
        delta_project_kernel,
        grid_spec=pltpu.PrefetchScalarGridSpec(
            num_scalar_prefetch=1,
            grid=(4,),
            in_specs=[pl.BlockSpec(pieces.shape, lambda i, sc: (0, 0, 0, 0)), weight, weight],
            out_specs=[pl.BlockSpec((CH, 512), lambda i, sc: (0, i))] * 4,
        ),
        out_shape=[jax.ShapeDtypeStruct((CH, 2048), BF16)] * 4,
        compiler_params=pltpu.CompilerParams(vmem_limit_bytes=VMEM),
        cost_estimate=cost(0.1),
        name="delta_project",
    )(scalars, pieces, own, other)


def pack_kernel(sc_ref, q_ref, g_ref, aw_ref, dw_ref, o0, o1, o2, o3, share_ref):
    for k, out in enumerate((o0, o1, o2, o3)):
        j = (sc_ref[0] + k) & 3
        out[:512, :256] = q_ref[j]
        out[:512, 256:] = g_ref[j]
        for n in range(4):
            out[512 + n * CH : 512 + (n + 1) * CH] = aw_ref[:, n * 512 : (n + 1) * 512]
    for n in range(4):
        share_ref[n * CH : (n + 1) * CH] = dw_ref[:, n * 512 : (n + 1) * 512]


def pack(scalars, query, gate, attn_weight, delta_weight):
    whole = pl.BlockSpec(query.shape, lambda i, sc: (0, 0, 0))
    half = pl.BlockSpec((CH, 2048), lambda i, sc: (sc[1], 0))
    return pl.pallas_call(
        pack_kernel,
        grid_spec=pltpu.PrefetchScalarGridSpec(
            num_scalar_prefetch=1,
            grid=(1,),
            in_specs=[whole, whole, half, half],
            out_specs=[pl.BlockSpec((1024, 512), lambda i, sc: (0, 0))] * 4
            + [pl.BlockSpec((512, 512), lambda i, sc: (0, 0))],
        ),
        out_shape=[jax.ShapeDtypeStruct((1024, 512), BF16)] * 4
        + [jax.ShapeDtypeStruct((512, 512), BF16)],
        compiler_params=pltpu.CompilerParams(vmem_limit_bytes=VMEM),
        cost_estimate=cost(0.1),
        name="pack_queries",
    )(scalars, query, gate, attn_weight, delta_weight)


def stack_kernel(r0, r1, r2, r3, out):
    for k, ref in enumerate((r0, r1, r2, r3)):
        out[k] = ref[...]


def stack_rows(arrays, block):
    return pl.pallas_call(
        stack_kernel,
        grid=(1,),
        in_specs=[pl.BlockSpec((512, 512), lambda i: (block, 0))] * 4,
        out_specs=pl.BlockSpec((4, 512, 512), lambda i: (0, 0, 0)),
        out_shape=jax.ShapeDtypeStruct((4, 512, 512), BF16),
        compiler_params=pltpu.CompilerParams(vmem_limit_bytes=VMEM),
        cost_estimate=cost(0.1),
        name="stack_weights",
    )(*arrays)


def select_kernel(src_ref, landed_ref, fresh_ref, out_ref):
    for j in range(4):
        out_ref[j, :CH] = landed_ref[src_ref[j], :CH]
        out_ref[j, CH:] = fresh_ref[j]


def select(source, landed, fresh):
    vmem = pl.BlockSpec(memory_space=pltpu.VMEM)
    return pl.pallas_call(
        select_kernel,
        in_specs=[pl.BlockSpec(memory_space=pltpu.SMEM), vmem, vmem],
        out_specs=vmem,
        out_shape=jax.ShapeDtypeStruct((4, CH + 64, 512), BF16),
        compiler_params=pltpu.CompilerParams(vmem_limit_bytes=VMEM),
        cost_estimate=cost(0.1),
        name="select_sessions",
    )(source, landed, fresh)


def attention_kernel(
    sc_ref, q0, q1, q2, q3, p0, p1, p2, p3, own_hbm, other_hbm, o0, o1, w_ref, w_sem, keys, values, heads
):
    fetches = [
        pltpu.make_async_copy(hbm, w_ref.at[n], w_sem.at[n])
        for n, hbm in enumerate((own_hbm, other_hbm))
    ]
    for fetch in fetches:
        fetch.start()
    y, length = sc_ref[1], sc_ref[2]
    rows = 2 * CH
    at_kept = lax.broadcasted_iota(jnp.int32, (1, 256), 1)
    at_fresh = lax.broadcasted_iota(jnp.int32, (1, 128), 1)
    kept_bias, fresh_place = [], []
    for e, ref in enumerate((p0, p1, p2, p3)):
        from_y = (y - e) & 3
        place = ((at_kept >> 6) * 4 + from_y) * 64 + (at_kept & 63)
        kept_bias.append(jnp.where(place < length, 0.0, NEG))
        fresh_place.append(((at_fresh >> 5) * 4 + from_y) * 32 + (at_fresh & 31))
        for j in range(4):
            kept_at, fresh_at = e * 256 + j * 64, 1024 + e * 128 + j * 32
            keys[kept_at : kept_at + 64] = ref[j, :64]
            values[kept_at : kept_at + 64] = ref[j, 64:128]
            keys[fresh_at : fresh_at + 32] = ref[j, 128:160]
            values[fresh_at : fresh_at + 32] = ref[j, 160:]
    kept_bias = jnp.concatenate(kept_bias, axis=1)
    fresh_place = jnp.concatenate(fresh_place, axis=1)
    token = lax.broadcasted_iota(jnp.int32, (rows, 512), 0) & (CH - 1)
    scale = math.log2(math.e) / 16.0

    def load(n, pair, cols):
        at = pl.ds(pl.multiple_of(sc_ref[3 + n] * CH, CH), CH)
        return jnp.concatenate([r[at, cols] for r in pair], axis=0)

    def score(n, pair):
        query = load(n, pair, slice(0, 256))
        return mm_nt(query, keys[:1024]), mm_nt(query, keys[1024:])

    groups = [(n, g) for n in range(2) for g in range(2)]
    pairs = ((q0, q1), (q2, q3))
    ahead = score(0, pairs[0])
    for step, (n, g) in enumerate(groups):
        kept, fresh = ahead
        if step + 1 < len(groups):
            ahead = score(groups[step + 1][0], pairs[groups[step + 1][1]])
        kept = kept + kept_bias
        fresh = jnp.where(fresh_place <= token + sc_ref[3 + n] * CH, fresh, NEG)
        peak = jnp.maximum(
            jnp.max(kept, axis=1, keepdims=True), jnp.max(fresh, axis=1, keepdims=True)
        )
        kept = jnp.exp2((kept - peak) * scale)
        fresh = jnp.exp2((fresh - peak) * scale)
        total = jnp.sum(kept, axis=1, keepdims=True) + jnp.sum(fresh, axis=1, keepdims=True)
        mixed = mm(kept.astype(BF16), values[:1024]) + mm(fresh.astype(BF16), values[1024:])
        gate = load(n, pairs[g], slice(256, 512)).astype(F32)
        gated = (mixed / (total * (1.0 + jnp.exp(-gate)))).astype(BF16)
        for i in range(2):
            k = 2 * g + i
            heads[n * CH : (n + 1) * CH, k * 256 : (k + 1) * 256] = gated[i * CH : (i + 1) * CH]
    for fetch in fetches:
        fetch.wait()
    gated = [swap_halves(sc_ref[5], heads[:, k * 256 : (k + 1) * 256]) for k in range(4)]
    for j in range(4):
        rows = slice(j * CH, (j + 1) * CH)
        out = sum(
            mm(gated[k], jnp.concatenate([w_ref[0, k, rows], w_ref[1, k, rows]], axis=0))
            for k in range(4)
        ).astype(BF16)
        o0[:, j * 512 : (j + 1) * 512] = out[:CH]
        o1[:, j * 512 : (j + 1) * 512] = out[CH:]


def attention(scalars, queries, positions, own, other):
    whole = lambda a: pl.BlockSpec(a.shape, lambda i, sc: (0,) * a.ndim)
    return pl.pallas_call(
        attention_kernel,
        grid_spec=pltpu.PrefetchScalarGridSpec(
            num_scalar_prefetch=1,
            grid=(1,),
            in_specs=[pl.BlockSpec((512, 512), lambda i, sc: (0, 0))] * 4
            + [whole(a) for a in positions]
            + [pl.BlockSpec(memory_space=pl.ANY)] * 2,
            out_specs=[pl.BlockSpec((CH, 2048), lambda i, sc: (0, 0))] * 2,
            scratch_shapes=[
                pltpu.VMEM((2, 4, 512, 512), BF16),
                pltpu.SemaphoreType.DMA((2,)),
                pltpu.VMEM((1536, 256), BF16),
                pltpu.VMEM((1536, 256), BF16),
                pltpu.VMEM((2 * CH, 1024), BF16),
            ],
        ),
        out_shape=[jax.ShapeDtypeStruct((CH, 2048), BF16)] * 2,
        compiler_params=pltpu.CompilerParams(vmem_limit_bytes=VMEM),
        cost_estimate=cost(0.1),
        name="attention_project",
    )(scalars, *queries, *positions, own, other)


ORDER = (2, 1, 3)


def shift(array, axis, by):
    return lax.ppermute(array, axis, [(i, (i + by) % 4) for i in range(4)])


def row_of(array, index):
    return lax.dynamic_index_in_dim(array, index, 0, keepdims=False)


def all_to_all(array, axis):
    return lax.all_to_all(array, axis, split_axis=0, concat_axis=0, tiled=True)


def sum_over(parts, axis):
    total = parts[0].astype(F32)
    for piece in [shift(parts[d], axis, d) for d in ORDER]:
        total = total + piece.astype(F32)
    return total.astype(BF16)


def regroup(k):
    pairs = []
    for x in range(4):
        for y in range(4):
            a = 2 * (x % 2) + y % 2
            pairs.append((4 * x + y, 4 * ((a + k) % 4) + x // 2 + 2 * (y // 2)))
    return pairs


def on_device(
    delta_query,
    delta_key,
    delta_value,
    delta_gate,
    write_strength,
    decay_log,
    kept_state,
    kept_kv,
    fresh_kv,
    attn_query,
    attn_gate,
    cached_len,
    slot_of_session,
    delta_out_weight,
    attn_out_weight,
):
    count = attn_query.shape[0]
    owners = 8
    owner_id = lax.axis_index(("z", "core"))
    x, y, core = lax.axis_index("x"), lax.axis_index("y"), lax.axis_index("core")
    session_ids = jnp.arange(slot_of_session.shape[0], dtype=jnp.int32)
    on_mine = slot_of_session // count == owner_id
    owner_of = session_ids // count
    wanted = on_mine[None, :] & (owner_of[None, :] == jnp.arange(owners, dtype=jnp.int32)[:, None])
    picked_slot = jnp.sum(jnp.where(wanted, slot_of_session[None, :] - owner_id * count, 0), axis=1)
    source = lax.dynamic_slice_in_dim(slot_of_session, owner_id * count, count) // count
    length = lax.dynamic_index_in_dim(cached_len, owner_id * count + x, 0, keepdims=False)
    source = source.astype(jnp.int32)

    kept_rows = kept_kv.transpose(0, 2, 1, 3).reshape(count, 128, 512)
    state_rows = kept_state.astype(BF16).reshape(count, 2, 4, 32, 128)
    state_rows = state_rows.transpose(0, 1, 3, 2, 4).reshape(count, 64, 512)
    leaving = jnp.take(jnp.concatenate([kept_rows, state_rows], axis=1), picked_slot, axis=0)
    landed = all_to_all(leaving, ("z", "core"))

    place = jnp.stack([2 * (x & 1) + (y & 1), core]).astype(jnp.int32)
    *blocks, delta_share = pack(
        after(place, leaving), attn_query, attn_gate, attn_out_weight, delta_out_weight
    )
    queries = [lax.ppermute(blocks[k], ("x", "y"), regroup(k)) for k in range(4)]

    delta_key = after(delta_key, leaving, *blocks)
    prepared = prep(delta_query, delta_key, delta_value, write_strength, decay_log)
    landed = after(landed, prepared)

    fresh_rows = fresh_kv.transpose(0, 2, 1, 3).reshape(count, 64, 512)
    chosen = select(source, landed, fresh_rows)
    rows = all_to_all(chosen, "x")
    delta_share = after(delta_share, chosen)
    delta_own = [delta_share] + [shift(delta_share, "y", d) for d in (1, 2, 3)]

    delta_heads, final_state = scan(after(source, chosen), landed, prepared, delta_gate)
    attn_own = stack_rows(queries, 1)
    rows = after(rows, delta_heads, attn_own)

    def swap_cores(array):
        return lax.ppermute(array, "core", [(0, 1), (1, 0)])

    attn_other = swap_cores(attn_own)

    def columns(target):
        return lax.dynamic_slice_in_dim(rows, (target & 1) * 256, 256, 2)

    parts = [columns(y + d) for d in range(4)]
    positions = [parts[0]] + [shift(parts[d], "y", d) for d in (1, 2, 3)]

    pieces = all_to_all(after(delta_heads, positions), "y")
    delta_own = stack_rows(after(delta_own, positions), 0)
    delta_other = swap_cores(delta_own)

    def quarters(first, second, *others):
        asked = jnp.stack([x, y, length, (y + first) & 3, (y + second) & 3, core])
        return attention(
            after(asked.astype(jnp.int32), *others), queries, positions, attn_own, attn_other
        )

    two, one = quarters(2, 1)
    scalars = jnp.stack([x, y, core]).astype(jnp.int32)
    delta_parts = delta_project(scalars, after(pieces, two), delta_own, delta_other)
    three, last = quarters(3, 0, delta_parts)
    delta_mixed = sum_over(delta_parts, "x")
    attn_mixed = sum_over([last, one, two, three], "y")
    return (delta_mixed, attn_mixed, final_state)


def solution(mesh):
    split = Mesh(np.asarray(mesh.devices).reshape(4, 2, 4, 4), ("z", "core", "x", "y"))
    cache, head = ("z", "core"), ("x", "y")
    in_specs = (
        P(cache, None, head),
        P(cache, None, head),
        P(cache, None, head),
        P(cache, None, head),
        P(cache, head, None),
        P(cache, head, None),
        P(cache, head, None, None),
        P(cache, head, None, None),
        P(cache, head, None, None),
        P(cache, None, head),
        P(cache, None, head),
        P(),
        P(),
        P(head, None),
        P(head, None),
    )
    out_specs = (
        P(cache + head, None),
        P(cache + head, None),
        P(cache, head, None, None),
    )
    return jax.shard_map(
        on_device, mesh=split, in_specs=in_specs, out_specs=out_specs, check_vma=False
    )
```

time: 390 us -> 197 us (0.51)
  matrix products: 139 us -> 0 us
  waiting for transfers between devices: 154 us -> 65.3 us
  Pallas kernels: 0 us -> 57.8 us
  starting transfers between devices: 9.3 us -> 55.3 us
  local copies, waits for them, and re-layouts: 36.1 us -> 7.79 us
  other arithmetic: 35 us -> 8.1 us
  between operations: 14.1 us -> 0.88 us
    reduce_scatter x2 -> x0, waiting for transfers between devices: 145 us -> none  [the longest x1 88.2 us: on_device(): lax.psum_scatter(jnp.dot(taken, attn_out_weight, preferred_element_type=j...]
    dot_general x158 -> x0, matrix products: 139 us -> none  [the longest x48 18.7 us: advance(): inverse = jnp.matmul(inverse, identity_block + power, precision=highest)]
    ppermute x0 -> x18, waiting for transfers between devices: none -> 60.3 us  [the longest x12 40.3 us: shift(): return lax.ppermute(array, axis, [(i, (i + by) % 4) for i in range(4)])]
    pallas_call x0 -> x9, Pallas kernels: none -> 57.8 us  [the longest x2 17 us: attention(): pl.pallas_call(attention_kernel, grid_spec=pltpu.PrefetchScalarGridSpec(n...]
    ppermute x0 -> x18, starting transfers between devices: none -> 40.6 us  [the longest x12 25.9 us: shift(): return lax.ppermute(array, axis, [(i, (i + by) % 4) for i in range(4)])]
    mul x17 -> x0, other arithmetic: 10.1 us -> none  [the longest x8 8.71 us: advance(): b_blk[..., None] * growth * k_blk]
    transpose x3 -> x1, local copies, waits for them, and re-layouts: 9.89 us -> 0.74 us  [on_device(): fresh_rows = fresh_kv.transpose(0, 2, 1, 3).reshape(count, 64, 512)]
    gather x4 -> x1, local copies, waits for them, and re-layouts: 7.94 us -> 0.65 us  [on_device(): jnp.take(jnp.concatenate([kept_rows, state_rows], axis=1), picked_slot, a...]
  transfers between devices with their start and end apart: 6 -> 21, of which waited for: 4 -> 9; matrix products, arithmetic and copies ran while one was open for 53% -> 4% of each run, Pallas kernels for 0% -> 26%
where the time goes in v1:
time: 197 us; the launch traced here: 195 us
  waiting for transfers between devices  65.3 us (33%)
  Pallas kernels  57.8 us (29%)
  starting transfers between devices  55.3 us (28%)
  other arithmetic  8.1 us (4%)
  local copies, waits for them, and re-layouts  7.79 us (4%)
    ppermute x12, waiting for transfers between devices, shift(): return lax.ppermute(array, axis, [(i, (i + by) % 4) for i in range(4)])  40.3 us
    ppermute x12, starting transfers between devices, shift(): return lax.ppermute(array, axis, [(i, (i + by) % 4) for i in range(4)])  25.9 us
    ppermute x4, waiting for transfers between devices, on_device(): lax.ppermute(blocks[k], ('x', 'y'), regroup(k))  20.1 us
    pallas_call x2, Pallas kernels, attention(): pl.pallas_call(attention_kernel, grid_spec=pltpu.PrefetchScalarGridSpec(n...  17 us
    all_to_all x3, starting transfers between devices, all_to_all(): return lax.all_to_all(array, axis, split_axis=0, concat_axis=0, tiled=True)  14.7 us
    ppermute x4, starting transfers between devices, on_device(): lax.ppermute(blocks[k], ('x', 'y'), regroup(k))  14.6 us
    pallas_call x1, Pallas kernels, prep(): pl.pallas_call(prep_kernel, grid=(chunks,), in_specs=[spec_tok(CH), spec_...  13.7 us
    pallas_call x1, Pallas kernels, scan(): pl.pallas_call(scan_kernel, grid_spec=pltpu.PrefetchScalarGridSpec(num_sc...  7.1 us
  transfers between devices with their start and end apart: 21, of which 9 were waited for; matrix products, arithmetic and copies ran while one was open for 4% of the time, Pallas kernels for 26%

profile of v1, /device:TPU:0, one launch (start us, length us, event | category | flops | bytes accessed | tf_op | source)
XLA Modules:
  0.0 195.2 jit_solution(3838201768007567336)
XLA Ops:
  5.7 5.4 %all-to-all-start = ((bf16[8,192,512]{2,1,0:T(8,128)(2,1)}), bf16[8,192,512]{2,1,0:T(8,128)(2,1)S(1)}, u32[]{:S(2)}, u32[]{:S(2)}) async-start(bf16[8,192,512]{2,1,0:T(8,128)(2,1)} %broadcast_select_fusion), calls=%async_computation | async-start | bytes 3145728 | tf_op jit(solution)/shard_map/all_to_all | solution.py:416
  11.6 4.9 %pack_queries.1 = (bf16[1024,512]{1,0:T(8,128)(2,1)}, bf16[1024,512]{1,0:T(8,128)(2,1)}, bf16[1024,512]{1,0:T(8,128)(2,1)}, bf16[1024,512]{1,0:T(8,128)(2,1)}, bf16[512,512]{1,0:T(8,128)(2,1)}) custom-call(s32[2]{0:T(128)} %pad_add_fusion.1.sc_ref, bf16[4,512,256]{2,1,0:T(8,128)(2,1)} %q_ref.2, bf16[4,512,256]{2,1,0:T(8,128)(2,1)} %g_ref.2, ...), custom_call_target="tpu_custom_call" | custom-call | flops 100000000 | bytes 300000 | tf_op jit(solution)/shard_map/pack_queries/pallas_call | solution.py:252
  18.6 4.9 %collective-permute-start.1 = (bf16[1024,512]{1,0:T(8,128)(2,1)}, bf16[1024,512]{1,0:T(8,128)(2,1)}, u32[]{:S(2)}, u32[]{:S(2)}) collective-permute-start(bf16[1024,512]{1,0:T(8,128)(2,1)} %get-tuple-element.38), channel_id=1, source_target_pairs={{0,4},{1,8},{2,6},{3,10},{4,12},{5,0},{6,14},{7,2},{8,5},{9,9},{10... | collective-permute-start | bytes 3145736 | tf_op jit(solution)/shard_map/ppermute | solution.py:475
  23.5 3.7 %collective-permute-start.2 = (bf16[1024,512]{1,0:T(8,128)(2,1)}, bf16[1024,512]{1,0:T(8,128)(2,1)}, u32[]{:S(2)}, u32[]{:S(2)}) collective-permute-start(bf16[1024,512]{1,0:T(8,128)(2,1)} %get-tuple-element.39), channel_id=1, source_target_pairs={{0,8},{1,12},{2,10},{3,14},{4,0},{5,4},{6,2},{7,6},{8,9},{9,13},{1... | collective-permute-start | bytes 3145736 | tf_op jit(solution)/shard_map/ppermute | solution.py:475
  27.2 4.0 %collective-permute-start.3 = (bf16[1024,512]{1,0:T(8,128)(2,1)}, bf16[1024,512]{1,0:T(8,128)(2,1)}, u32[]{:S(2)}, u32[]{:S(2)}) collective-permute-start(bf16[1024,512]{1,0:T(8,128)(2,1)} %get-tuple-element.40), channel_id=1, source_target_pairs={{0,12},{1,0},{2,14},{3,2},{4,4},{5,8},{6,6},{7,10},{8,13},{9,1},{1... | collective-permute-start | bytes 3145736 | tf_op jit(solution)/shard_map/ppermute | solution.py:475
  31.9 13.7 %delta_prep.1 = (bf16[4,8,256,128]{3,2,1,0:T(8,128)(2,1)}, f32[4,8,128,128]{3,2,1,0:T(8,128)}, bf16[4,8,128,128]{3,2,1,0:T(8,128)(2,1)}, bf16[4,8,128,128]{3,2,1,0:T(8,128)(2,1)}, f32[4,8,128]{2,1,0:T(8,128)}) custom-call(bf16[4,512,128]{2,1,0:T(8,128)(2,1)} %q_ref.3, bf16[4,512,128]{2,1,0:T(8,128)(2,1)} %k_ref, bf16[4,512,256]{2,1,0:T(8,128)(2,1)} %v_ref.1, ...), custom_call_target="tpu_custom_call" | custom-call | flops 100000000 | bytes 300000 | tf_op jit(solution)/shard_map/delta_prep/pallas_call | solution.py:110
  49.8 5.6 %all-to-all-start.1 = ((bf16[4,192,512]{2,1,0:T(8,128)(2,1)}), bf16[4,192,512]{2,1,0:T(8,128)(2,1)S(1)}, u32[]{:S(2)}, u32[]{:S(2)}) async-start(bf16[4,192,512]{2,1,0:T(8,128)(2,1)} %select_sessions.1), calls=%async_computation.1 | async-start | bytes 1572864 | tf_op jit(solution)/shard_map/all_to_all | solution.py:416
  57.9 12.0 %collective-permute-done.1.r1.q1 = bf16[1024,512]{1,0:T(8,128)(2,1)} collective-permute-done((bf16[1024,512]{1,0:T(8,128)(2,1)}, bf16[1024,512]{1,0:T(8,128)(2,1)}, u32[]{:S(2)}, u32[]{:S(2)}) %collective-permute-start.1) | collective-permute-done | bytes 1048608 | tf_op jit(solution)/shard_map/ppermute | solution.py:475
  72.7 5.2 %collective-permute-done.3.r3.q3 = bf16[1024,512]{1,0:T(8,128)(2,1)} collective-permute-done((bf16[1024,512]{1,0:T(8,128)(2,1)}, bf16[1024,512]{1,0:T(8,128)(2,1)}, u32[]{:S(2)}, u32[]{:S(2)}) %collective-permute-start.3) | collective-permute-done | bytes 1048608 | tf_op jit(solution)/shard_map/ppermute | solution.py:475
  77.9 3.0 %stack_weights.2.own_hbm = bf16[4,512,512]{2,1,0:T(8,128)(2,1)} custom-call(bf16[1024,512]{1,0:T(8,128)(2,1)} %copy-done.2, bf16[1024,512]{1,0:T(8,128)(2,1)} %collective-permute-done.1.r1.q1, bf16[1024,512]{1,0:T(8,128)(2,1)} %collective-permute-done.2.r2.q2, bf16[1024,512]{1,0:T(8,128)(2,1)} %collective-permute-done.3.r3.q3), custom_call_target="tpu_custom_call" | custom-call | flops 100000000 | bytes 300000 | tf_op jit(solution)/shard_map/stack_weights/pallas_call | solution.py:275
  85.9 7.1 %delta_scan.1 = (bf16[4,4,128,256]{3,2,1,0:T(8,128)(2,1)}, f32[4,2,128,128]{3,2,1,0:T(8,128)}) custom-call(s32[4]{0:T(128)} %and_select_fusion.2.src_ref, bf16[8,192,512]{2,1,0:T(8,128)(2,1)} %copy-done.1, bf16[4,8,256,128]{3,2,1,0:T(8,128)(2,1)} %get-tuple-element.42.wq_ref, f32[4,8,128,128]{3,2,1,0:T(8,128)} %get-tuple-element.43.u_ref, ...), custom_call_target="tpu_custom_call" | custom-call | flops 100000000 | bytes 300000 | tf_op jit(solution)/shard_map/delta_scan/pallas_call | solution.py:171
  97.2 13.2 %collective-permute-done.9.r2 = bf16[512,512]{1,0:T(8,128)(2,1)} collective-permute-done((bf16[512,512]{1,0:T(8,128)(2,1)}, bf16[512,512]{1,0:T(8,128)(2,1)}, u32[]{:S(2)}, u32[]{:S(2)}) %collective-permute-start.9) | collective-permute-done | bytes 524320 | tf_op jit(solution)/shard_map/ppermute | solution.py:408
  110.3 5.9 %collective-permute-done.4.p1 = bf16[4,192,256]{2,1,0:T(8,128)(2,1)S(1)} collective-permute-done((bf16[4,192,256]{2,1,0:T(8,128)(2,1)S(1)}, bf16[4,192,256]{2,1,0:T(8,128)(2,1)S(1)}, u32[]{:S(2)}, u32[]{:S(2)}) %collective-permute-start.4) | collective-permute-done | bytes 393248 | tf_op jit(solution)/shard_map/ppermute | solution.py:408
  116.2 9.2 %collective-permute-done.5.p2 = bf16[4,192,256]{2,1,0:T(8,128)(2,1)S(1)} collective-permute-done((bf16[4,192,256]{2,1,0:T(8,128)(2,1)S(1)}, bf16[4,192,256]{2,1,0:T(8,128)(2,1)S(1)}, u32[]{:S(2)}, u32[]{:S(2)}) %collective-permute-start.5) | collective-permute-done | bytes 393248 | tf_op jit(solution)/shard_map/ppermute | solution.py:408
  125.4 3.3 %stack_weights.3.own_ref = bf16[4,512,512]{2,1,0:T(8,128)(2,1)} custom-call(bf16[512,512]{1,0:T(8,128)(2,1)} %get-tuple-element.56.r0, bf16[512,512]{1,0:T(8,128)(2,1)} %collective-permute-done.8.r1, bf16[512,512]{1,0:T(8,128)(2,1)} %collective-permute-done.9.r2, bf16[512,512]{1,0:T(8,128)(2,1)} %collective-permute-done.10.r3), custom_call_target="tpu_custom_call" | custom-call | flops 100000000 | bytes 300000 | tf_op jit(solution)/shard_map/stack_weights/pallas_call | solution.py:275
  128.8 3.7 %all-to-all-start.2 = ((bf16[4,4,128,256]{3,2,1,0:T(8,128)(2,1)}), bf16[4,4,128,256]{3,2,1,0:T(8,128)(2,1)S(1)}, u32[]{:S(2)}, u32[]{:S(2)}) async-start(bf16[4,4,128,256]{3,2,1,0:T(8,128)(2,1)} %get-tuple-element.51), calls=%async_computation.2 | async-start | bytes 2097152 | tf_op jit(solution)/shard_map/all_to_all | solution.py:416
  134.9 8.4 %attention_project.2 = (bf16[128,2048]{1,0:T(8,128)(2,1)}, bf16[128,2048]{1,0:T(8,128)(2,1)}) custom-call(s32[6]{0:T(128)} %stack.53.sc_ref, bf16[1024,512]{1,0:T(8,128)(2,1)} %copy-done.2, bf16[1024,512]{1,0:T(8,128)(2,1)} %collective-permute-done.1.r1.q1, bf16[1024,512]{1,0:T(8,128)(2,1)} %collective-permute-done.2.r2.q2, ...), custom_call_target="tpu_custom_call" | custom-call | flops 100000000 | bytes 300000 | tf_op jit(solution)/shard_map/attention_project/pallas_call | solution.py:380
  143.3 5.0 %all-to-all-done.2.heads_ref = bf16[4,4,128,256]{3,2,1,0:T(8,128)(2,1)S(1)} async-done(((bf16[4,4,128,256]{3,2,1,0:T(8,128)(2,1)}), bf16[4,4,128,256]{3,2,1,0:T(8,128)(2,1)S(1)}, u32[]{:S(2)}, u32[]{:S(2)}) %all-to-all-start.2) | async-done | bytes 1048608 | tf_op jit(solution)/shard_map/all_to_all | solution.py:416
  149.3 6.5 %delta_project.1 = (bf16[128,2048]{1,0:T(8,128)(2,1)}, bf16[128,2048]{1,0:T(8,128)(2,1)}, bf16[128,2048]{1,0:T(8,128)(2,1)}, bf16[128,2048]{1,0:T(8,128)(2,1)}) custom-call(s32[3]{0:T(128)} %pad_add_fusion.sc_ref, bf16[4,4,128,256]{3,2,1,0:T(8,128)(2,1)} %copy-done.3, bf16[4,512,512]{2,1,0:T(8,128)(2,1)} %stack_weights.3.own_ref, ...), custom_call_target="tpu_custom_call" | custom-call | flops 100000000 | bytes 300000 | tf_op jit(solution)/shard_map/delta_project/pallas_call | solution.py:223
  155.8 8.2 %collective-permute-start.12 = (bf16[128,2048]{1,0:T(8,128)(2,1)}, bf16[128,2048]{1,0:T(8,128)(2,1)S(1)}, u32[]{:S(2)}, u32[]{:S(2)}) collective-permute-start(bf16[128,2048]{1,0:T(8,128)(2,1)} %get-tuple-element.61), channel_id=1, source_target_pairs={{0,8},{4,12},{8,0},{12,4},{1,9},{5,13},{9,1},{13,5},{2,10},{6,14},... | collective-permute-start | bytes 1572872 | tf_op jit(solution)/shard_map/ppermute | solution.py:408
  163.9 3.2 %collective-permute-start.14 = (bf16[128,2048]{1,0:T(8,128)(2,1)}, bf16[128,2048]{1,0:T(8,128)(2,1)S(1)}, u32[]{:S(2)}, u32[]{:S(2)}) collective-permute-start(bf16[128,2048]{1,0:T(8,128)(2,1)} %get-tuple-element.63), channel_id=1, source_target_pairs={{0,12},{4,0},{8,4},{12,8},{1,13},{5,1},{9,5},{13,9},{2,14},{6,2},{... | collective-permute-start | bytes 1572872 | tf_op jit(solution)/shard_map/ppermute | solution.py:408
  170.4 8.6 %attention_project.3 = (bf16[128,2048]{1,0:T(8,128)(2,1)}, bf16[128,2048]{1,0:T(8,128)(2,1)}) custom-call(s32[6]{0:T(128)} %stack.56.sc_ref, bf16[1024,512]{1,0:T(8,128)(2,1)} %copy-done.2, bf16[1024,512]{1,0:T(8,128)(2,1)} %collective-permute-done.1.r1.q1, bf16[1024,512]{1,0:T(8,128)(2,1)} %collective-permute-done.2.r2.q2, ...), custom_call_target="tpu_custom_call" | custom-call | flops 100000000 | bytes 300000 | tf_op jit(solution)/shard_map/attention_project/pallas_call | solution.py:380
  180.9 6.3 %collective-permute-done.13 = bf16[128,2048]{1,0:T(8,128)(2,1)S(1)} collective-permute-done((bf16[128,2048]{1,0:T(8,128)(2,1)}, bf16[128,2048]{1,0:T(8,128)(2,1)S(1)}, u32[]{:S(2)}, u32[]{:S(2)}) %collective-permute-start.13) | collective-permute-done | bytes 524320 | tf_op jit(solution)/shard_map/ppermute | solution.py:408
  188.3 5.8 %collective-permute-done.16 = bf16[128,2048]{1,0:T(8,128)(2,1)S(1)} collective-permute-done((bf16[128,2048]{1,0:T(8,128)(2,1)}, bf16[128,2048]{1,0:T(8,128)(2,1)S(1)}, u32[]{:S(2)}, u32[]{:S(2)}) %collective-permute-start.16) | collective-permute-done | bytes 524320 | tf_op jit(solution)/shard_map/ppermute | solution.py:408
  (76 shorter events, 37.8 us)
Async XLA Ops:
  5.7 40.6 %all-to-all-start = ((bf16[8,192,512]{2,1,0:T(8,128)(2,1)}), bf16[8,192,512]{2,1,0:T(8,128)(2,1)S(1)}, u32[]{:S(2)}, u32[]{:S(2)}) async-start(bf16[8,192,512]{2,1,0:T(8,128)(2,1)} %broadcast_select_fusion), calls=%async_computation | async-start | bytes 3145728 | tf_op jit(solution)/shard_map/all_to_all | solution.py:416
  11.6 19.5 %copy-start.10 = (bf16[4,32,2,512]{3,2,1,0:T(2,128)(2,1)S(1)}, bf16[4,32,2,512]{3,2,1,0:T(2,128)(2,1)}, u32[]{:S(2)}) copy-start(bf16[4,32,2,512]{3,2,1,0:T(2,128)(2,1)} %param.23) | copy-start | bytes 786436
  16.6 29.0 %copy-start.11 = (s32[32]{0:T(128)S(1)}, s32[32]{0:T(128)}, u32[]{:S(2)}) copy-start(s32[32]{0:T(128)} %param.27) | copy-start | bytes 388
  16.6 41.3 %collective-permute-start = (bf16[1024,512]{1,0:T(8,128)(2,1)}, bf16[1024,512]{1,0:T(8,128)(2,1)S(1)}, u32[]{:S(2)}, u32[]{:S(2)}) collective-permute-start(bf16[1024,512]{1,0:T(8,128)(2,1)} %get-tuple-element.37), channel_id=1, source_target_pairs={{0,0},{1,4},{2,2},{3,6},{4,8},{5,12},{6,10},{7,14},{8,1},{9,5},{10... | collective-permute-start | bytes 3145736 | tf_op jit(solution)/shard_map/ppermute | solution.py:475
  18.6 51.3 %collective-permute-start.1 = (bf16[1024,512]{1,0:T(8,128)(2,1)}, bf16[1024,512]{1,0:T(8,128)(2,1)}, u32[]{:S(2)}, u32[]{:S(2)}) collective-permute-start(bf16[1024,512]{1,0:T(8,128)(2,1)} %get-tuple-element.38), channel_id=1, source_target_pairs={{0,4},{1,8},{2,6},{3,10},{4,12},{5,0},{6,14},{7,2},{8,5},{9,9},{10... | collective-permute-start | bytes 3145736 | tf_op jit(solution)/shard_map/ppermute | solution.py:475
  23.5 49.2 %collective-permute-start.2 = (bf16[1024,512]{1,0:T(8,128)(2,1)}, bf16[1024,512]{1,0:T(8,128)(2,1)}, u32[]{:S(2)}, u32[]{:S(2)}) collective-permute-start(bf16[1024,512]{1,0:T(8,128)(2,1)} %get-tuple-element.39), channel_id=1, source_target_pairs={{0,8},{1,12},{2,10},{3,14},{4,0},{5,4},{6,2},{7,6},{8,9},{9,13},{1... | collective-permute-start | bytes 3145736 | tf_op jit(solution)/shard_map/ppermute | solution.py:475
  27.2 50.7 %collective-permute-start.3 = (bf16[1024,512]{1,0:T(8,128)(2,1)}, bf16[1024,512]{1,0:T(8,128)(2,1)}, u32[]{:S(2)}, u32[]{:S(2)}) collective-permute-start(bf16[1024,512]{1,0:T(8,128)(2,1)} %get-tuple-element.40), channel_id=1, source_target_pairs={{0,12},{1,0},{2,14},{3,2},{4,4},{5,8},{6,6},{7,10},{8,13},{9,1},{1... | collective-permute-start | bytes 3145736 | tf_op jit(solution)/shard_map/ppermute | solution.py:475
  49.8 43.2 %all-to-all-start.1 = ((bf16[4,192,512]{2,1,0:T(8,128)(2,1)}), bf16[4,192,512]{2,1,0:T(8,128)(2,1)S(1)}, u32[]{:S(2)}, u32[]{:S(2)}) async-start(bf16[4,192,512]{2,1,0:T(8,128)(2,1)} %select_sessions.1), calls=%async_computation.1 | async-start | bytes 1572864 | tf_op jit(solution)/shard_map/all_to_all | solution.py:416
  55.4 40.8 %collective-permute-start.10 = (bf16[512,512]{1,0:T(8,128)(2,1)}, bf16[512,512]{1,0:T(8,128)(2,1)}, u32[]{:S(2)}, u32[]{:S(2)}) collective-permute-start(bf16[512,512]{1,0:T(8,128)(2,1)} %get-tuple-element.56.r0), channel_id=1, source_target_pairs={{0,3},{1,0},{2,1},{3,2},{4,7},{5,4},{6,5},{7,6},{8,11},{9,8},{10,9... | collective-permute-start | bytes 1572872 | tf_op jit(solution)/shard_map/ppermute | solution.py:408
  57.9 20.1 %copy-start.2 = (bf16[1024,512]{1,0:T(8,128)(2,1)}, bf16[1024,512]{1,0:T(8,128)(2,1)S(1)}, u32[]{:S(2)}) copy-start(bf16[1024,512]{1,0:T(8,128)(2,1)S(1)} %collective-permute-done.r0.q0) | copy-start | bytes 3145732
  80.9 16.2 %collective-permute-start.8 = (bf16[512,512]{1,0:T(8,128)(2,1)}, bf16[512,512]{1,0:T(8,128)(2,1)}, u32[]{:S(2)}, u32[]{:S(2)}) collective-permute-start(bf16[512,512]{1,0:T(8,128)(2,1)} %get-tuple-element.56.r0), channel_id=1, source_target_pairs={{0,1},{1,2},{2,3},{3,0},{4,5},{5,6},{6,7},{7,4},{8,9},{9,10},{10,1... | collective-permute-start | bytes 1572872 | tf_op jit(solution)/shard_map/ppermute | solution.py:408
  83.0 27.3 %collective-permute-start.9 = (bf16[512,512]{1,0:T(8,128)(2,1)}, bf16[512,512]{1,0:T(8,128)(2,1)}, u32[]{:S(2)}, u32[]{:S(2)}) collective-permute-start(bf16[512,512]{1,0:T(8,128)(2,1)} %get-tuple-element.56.r0), channel_id=1, source_target_pairs={{0,2},{1,3},{2,0},{3,1},{4,6},{5,7},{6,4},{7,5},{8,10},{9,11},{10,... | collective-permute-start | bytes 1572872 | tf_op jit(solution)/shard_map/ppermute | solution.py:408
  93.9 22.3 %collective-permute-start.4 = (bf16[4,192,256]{2,1,0:T(8,128)(2,1)S(1)}, bf16[4,192,256]{2,1,0:T(8,128)(2,1)S(1)}, u32[]{:S(2)}, u32[]{:S(2)}) collective-permute-start(bf16[4,192,256]{2,1,0:T(8,128)(2,1)S(1)} %get-tuple-element.71), channel_id=1, source_target_pairs={{0,1},{1,2},{2,3},{3,0},{4,5},{5,6},{6,7},{7,4},{8,9},{9,10},{10,1... | collective-permute-start | bytes 1179656 | tf_op jit(solution)/shard_map/ppermute | solution.py:408
  93.9 31.5 %collective-permute-start.5 = (bf16[4,192,256]{2,1,0:T(8,128)(2,1)S(1)}, bf16[4,192,256]{2,1,0:T(8,128)(2,1)S(1)}, u32[]{:S(2)}, u32[]{:S(2)}) collective-permute-start(bf16[4,192,256]{2,1,0:T(8,128)(2,1)S(1)} %get-tuple-element.70), channel_id=1, source_target_pairs={{0,2},{1,3},{2,0},{3,1},{4,6},{5,7},{6,4},{7,5},{8,10},{9,11},{10,... | collective-permute-start | bytes 1179656 | tf_op jit(solution)/shard_map/ppermute | solution.py:408
  96.2 29.2 %collective-permute-start.6 = (bf16[4,192,256]{2,1,0:T(8,128)(2,1)S(1)}, bf16[4,192,256]{2,1,0:T(8,128)(2,1)S(1)}, u32[]{:S(2)}, u32[]{:S(2)}) collective-permute-start(bf16[4,192,256]{2,1,0:T(8,128)(2,1)S(1)} %get-tuple-element.69), channel_id=1, source_target_pairs={{0,3},{1,0},{2,1},{3,2},{4,7},{5,4},{6,5},{7,6},{8,11},{9,8},{10,9... | collective-permute-start | bytes 1179656 | tf_op jit(solution)/shard_map/ppermute | solution.py:408
  97.2 37.8 %collective-permute-start.7 = (bf16[4,512,512]{2,1,0:T(8,128)(2,1)S(1)}, bf16[4,512,512]{2,1,0:T(8,128)(2,1)}, u32[]{:S(2)}, u32[]{:S(2)}) collective-permute-start(bf16[4,512,512]{2,1,0:T(8,128)(2,1)S(1)} %copy-done), channel_id=1, source_target_pairs={{0,16},{16,0},{1,17},{17,1},{2,18},{18,2},{3,19},{19,3},{4,20},{20... | collective-permute-start | bytes 6291464 | tf_op jit(solution)/shard_map/ppermute | solution.py:492
  128.7 19.6 %collective-permute-start.11 = (bf16[4,512,512]{2,1,0:T(8,128)(2,1)}, bf16[4,512,512]{2,1,0:T(8,128)(2,1)}, u32[]{:S(2)}, u32[]{:S(2)}) collective-permute-start(bf16[4,512,512]{2,1,0:T(8,128)(2,1)} %stack_weights.3.own_ref), channel_id=1, source_target_pairs={{0,16},{16,0},{1,17},{17,1},{2,18},{18,2},{3,19},{19,3},{4,20},{20... | collective-permute-start | bytes 6291464 | tf_op jit(solution)/shard_map/ppermute | solution.py:492
  128.8 19.5 %all-to-all-start.2 = ((bf16[4,4,128,256]{3,2,1,0:T(8,128)(2,1)}), bf16[4,4,128,256]{3,2,1,0:T(8,128)(2,1)S(1)}, u32[]{:S(2)}, u32[]{:S(2)}) async-start(bf16[4,4,128,256]{3,2,1,0:T(8,128)(2,1)} %get-tuple-element.51), calls=%async_computation.2 | async-start | bytes 2097152 | tf_op jit(solution)/shard_map/all_to_all | solution.py:416
  155.8 23.3 %collective-permute-start.12 = (bf16[128,2048]{1,0:T(8,128)(2,1)}, bf16[128,2048]{1,0:T(8,128)(2,1)S(1)}, u32[]{:S(2)}, u32[]{:S(2)}) collective-permute-start(bf16[128,2048]{1,0:T(8,128)(2,1)} %get-tuple-element.61), channel_id=1, source_target_pairs={{0,8},{4,12},{8,0},{12,4},{1,9},{5,13},{9,1},{13,5},{2,10},{6,14},... | collective-permute-start | bytes 1572872 | tf_op jit(solution)/shard_map/ppermute | solution.py:408
  163.9 23.2 %collective-permute-start.13 = (bf16[128,2048]{1,0:T(8,128)(2,1)}, bf16[128,2048]{1,0:T(8,128)(2,1)S(1)}, u32[]{:S(2)}, u32[]{:S(2)}) collective-permute-start(bf16[128,2048]{1,0:T(8,128)(2,1)} %get-tuple-element.62), channel_id=1, source_target_pairs={{0,4},{4,8},{8,12},{12,0},{1,5},{5,9},{9,13},{13,1},{2,6},{6,10},{... | collective-permute-start | bytes 1572872 | tf_op jit(solution)/shard_map/ppermute | solution.py:408
  163.9 23.2 %collective-permute-start.14 = (bf16[128,2048]{1,0:T(8,128)(2,1)}, bf16[128,2048]{1,0:T(8,128)(2,1)S(1)}, u32[]{:S(2)}, u32[]{:S(2)}) collective-permute-start(bf16[128,2048]{1,0:T(8,128)(2,1)} %get-tuple-element.63), channel_id=1, source_target_pairs={{0,12},{4,0},{8,4},{12,8},{1,13},{5,1},{9,5},{13,9},{2,14},{6,2},{... | collective-permute-start | bytes 1572872 | tf_op jit(solution)/shard_map/ppermute | solution.py:408
  168.4 19.9 %collective-permute-start.15 = (bf16[128,2048]{1,0:T(8,128)(2,1)}, bf16[128,2048]{1,0:T(8,128)(2,1)S(1)}, u32[]{:S(2)}, u32[]{:S(2)}) collective-permute-start(bf16[128,2048]{1,0:T(8,128)(2,1)} %get-tuple-element.52), channel_id=1, source_target_pairs={{0,2},{1,3},{2,0},{3,1},{4,6},{5,7},{6,4},{7,5},{8,10},{9,11},{10,... | collective-permute-start | bytes 1572872 | tf_op jit(solution)/shard_map/ppermute | solution.py:408
  168.9 25.1 %collective-permute-start.16 = (bf16[128,2048]{1,0:T(8,128)(2,1)}, bf16[128,2048]{1,0:T(8,128)(2,1)S(1)}, u32[]{:S(2)}, u32[]{:S(2)}) collective-permute-start(bf16[128,2048]{1,0:T(8,128)(2,1)} %get-tuple-element.66), channel_id=1, source_target_pairs={{0,1},{1,2},{2,3},{3,0},{4,5},{5,6},{6,7},{7,4},{8,9},{9,10},{10,1... | collective-permute-start | bytes 1572872 | tf_op jit(solution)/shard_map/ppermute | solution.py:408
  179.0 15.0 %collective-permute-start.17 = (bf16[128,2048]{1,0:T(8,128)(2,1)}, bf16[128,2048]{1,0:T(8,128)(2,1)S(1)}, u32[]{:S(2)}, u32[]{:S(2)}) collective-permute-start(bf16[128,2048]{1,0:T(8,128)(2,1)} %get-tuple-element.67), channel_id=1, source_target_pairs={{0,3},{1,0},{2,1},{3,2},{4,7},{5,4},{6,5},{7,6},{8,11},{9,8},{10,9... | collective-permute-start | bytes 1572872 | tf_op jit(solution)/shard_map/ppermute | solution.py:408
  (10 other events, 63.8 us)

commit v2 on v1

--- a/solution.py
+++ b/solution.py
@@ -205,11 +205,11 @@
     )
 
 
-def delta_project_kernel(sc_ref, heads_ref, own_ref, other_ref, *outs):
-    x, y, core = sc_ref[0], sc_ref[1], sc_ref[2]
+def delta_project_kernel(sc_ref, h0, h1, h2, h3, own_ref, other_ref, *outs):
+    x, core = sc_ref[0], sc_ref[1]
     total = None
-    for e in range(4):
-        rows = jnp.concatenate([heads_ref[(y - e) & 3, (x + d) & 3] for d in range(4)], axis=0)
+    for e, heads_ref in enumerate((h0, h1, h2, h3)):
+        rows = jnp.concatenate([heads_ref[(x + d) & 3] for d in range(4)], axis=0)
         weight = jnp.concatenate([own_ref[e], other_ref[e]], axis=0)
         part = mm(swap_halves(core, rows), weight)
         total = part if total is None else total + part
@@ -225,40 +225,44 @@
         grid_spec=pltpu.PrefetchScalarGridSpec(
             num_scalar_prefetch=1,
             grid=(4,),
-            in_specs=[pl.BlockSpec(pieces.shape, lambda i, sc: (0, 0, 0, 0)), weight, weight],
+            in_specs=[pl.BlockSpec((4, CH, 2 * CH), lambda i, sc: (0, 0, 0))] * 4 + [weight, weight],
             out_specs=[pl.BlockSpec((CH, 512), lambda i, sc: (0, i))] * 4,
         ),
         out_shape=[jax.ShapeDtypeStruct((CH, 2048), BF16)] * 4,
         compiler_params=pltpu.CompilerParams(vmem_limit_bytes=VMEM),
         cost_estimate=cost(0.1),
         name="delta_project",
-    )(scalars, pieces, own, other)
-
-
-def pack_kernel(sc_ref, q_ref, g_ref, aw_ref, dw_ref, o0, o1, o2, o3, share_ref):
+    )(scalars, *pieces, own, other)
+
+
+def pack_kernel(sc_ref, q_ref, g_ref, aw_ref, dw_ref, o0, o1, o2, o3, delta_ref):
     for k, out in enumerate((o0, o1, o2, o3)):
         j = (sc_ref[0] + k) & 3
         out[:512, :256] = q_ref[j]
         out[:512, 256:] = g_ref[j]
         for n in range(4):
-            out[512 + n * CH : 512 + (n + 1) * CH] = aw_ref[:, n * 512 : (n + 1) * 512]
+            out[512 + n * 32 : 544 + n * 32] = aw_ref[:, n * 512 : (n + 1) * 512]
     for n in range(4):
-        share_ref[n * CH : (n + 1) * CH] = dw_ref[:, n * 512 : (n + 1) * 512]
+        delta_ref[n * CH : (n + 1) * CH] = dw_ref[:, n * 512 : (n + 1) * 512]
 
 
 def pack(scalars, query, gate, attn_weight, delta_weight):
     whole = pl.BlockSpec(query.shape, lambda i, sc: (0, 0, 0))
-    half = pl.BlockSpec((CH, 2048), lambda i, sc: (sc[1], 0))
     return pl.pallas_call(
         pack_kernel,
         grid_spec=pltpu.PrefetchScalarGridSpec(
             num_scalar_prefetch=1,
             grid=(1,),
-            in_specs=[whole, whole, half, half],
-            out_specs=[pl.BlockSpec((1024, 512), lambda i, sc: (0, 0))] * 4
+            in_specs=[
+                whole,
+                whole,
+                pl.BlockSpec((32, 2048), lambda i, sc: (sc[1] * 4 + sc[2], 0)),
+                pl.BlockSpec((CH, 2048), lambda i, sc: (sc[1], 0)),
+            ],
+            out_specs=[pl.BlockSpec((640, 512), lambda i, sc: (0, 0))] * 4
             + [pl.BlockSpec((512, 512), lambda i, sc: (0, 0))],
         ),
-        out_shape=[jax.ShapeDtypeStruct((1024, 512), BF16)] * 4
+        out_shape=[jax.ShapeDtypeStruct((640, 512), BF16)] * 4
         + [jax.ShapeDtypeStruct((512, 512), BF16)],
         compiler_params=pltpu.CompilerParams(vmem_limit_bytes=VMEM),
         cost_estimate=cost(0.1),
@@ -271,17 +275,39 @@
         out[k] = ref[...]
 
 
-def stack_rows(arrays, block):
+def stack_rows(arrays, rows, block):
     return pl.pallas_call(
         stack_kernel,
         grid=(1,),
-        in_specs=[pl.BlockSpec((512, 512), lambda i: (block, 0))] * 4,
-        out_specs=pl.BlockSpec((4, 512, 512), lambda i: (0, 0, 0)),
-        out_shape=jax.ShapeDtypeStruct((4, 512, 512), BF16),
+        in_specs=[pl.BlockSpec((rows, 512), lambda i: (block, 0))] * 4,
+        out_specs=pl.BlockSpec((4, rows, 512), lambda i: (0, 0, 0)),
+        out_shape=jax.ShapeDtypeStruct((4, rows, 512), BF16),
         compiler_params=pltpu.CompilerParams(vmem_limit_bytes=VMEM),
         cost_estimate=cost(0.1),
         name="stack_weights",
     )(*arrays)
+
+
+def merge_kernel(sc_ref, r0, r1, r2, r3, out):
+    for e, ref in enumerate((r0, r1, r2, r3)):
+        at = ((sc_ref[0] - e) & 3) * 32
+        for k in range(4):
+            for n in range(4):
+                rows = pl.ds(pl.multiple_of(n * CH + at, 32), 32)
+                out[k, rows] = ref[k, n * 32 : (n + 1) * 32]
+
+
+def merge_rows(z, arrays):
+    vmem = pl.BlockSpec(memory_space=pltpu.VMEM)
+    return pl.pallas_call(
+        merge_kernel,
+        in_specs=[pl.BlockSpec(memory_space=pltpu.SMEM)] + [vmem] * 4,
+        out_specs=vmem,
+        out_shape=jax.ShapeDtypeStruct((4, 512, 512), BF16),
+        compiler_params=pltpu.CompilerParams(vmem_limit_bytes=VMEM),
+        cost_estimate=cost(0.1),
+        name="merge_weights",
+    )(z, *arrays)
 
 
 def select_kernel(src_ref, landed_ref, fresh_ref, out_ref):
@@ -304,7 +330,7 @@
 
 
 def attention_kernel(
-    sc_ref, q0, q1, q2, q3, p0, p1, p2, p3, own_hbm, other_hbm, o0, o1, w_ref, w_sem, keys, values, heads
+    sc_ref, q0, q1, q2, q3, place_ref, own_hbm, other_hbm, o0, o1, w_ref, w_sem, keys, values, heads
 ):
     fetches = [
         pltpu.make_async_copy(hbm, w_ref.at[n], w_sem.at[n])
@@ -312,16 +338,16 @@
     ]
     for fetch in fetches:
         fetch.start()
-    y, length = sc_ref[1], sc_ref[2]
+    length = sc_ref[2]
     rows = 2 * CH
     at_kept = lax.broadcasted_iota(jnp.int32, (1, 256), 1)
     at_fresh = lax.broadcasted_iota(jnp.int32, (1, 128), 1)
     kept_bias, fresh_place = [], []
-    for e, ref in enumerate((p0, p1, p2, p3)):
-        from_y = (y - e) & 3
-        place = ((at_kept >> 6) * 4 + from_y) * 64 + (at_kept & 63)
+    for e in range(4):
+        ref = place_ref.at[e]
+        place = ((at_kept >> 6) * 4 + e) * 64 + (at_kept & 63)
         kept_bias.append(jnp.where(place < length, 0.0, NEG))
-        fresh_place.append(((at_fresh >> 5) * 4 + from_y) * 32 + (at_fresh & 31))
+        fresh_place.append(((at_fresh >> 5) * 4 + e) * 32 + (at_fresh & 31))
         for j in range(4):
             kept_at, fresh_at = e * 256 + j * 64, 1024 + e * 128 + j * 32
             keys[kept_at : kept_at + 64] = ref[j, :64]
@@ -383,7 +409,7 @@
             num_scalar_prefetch=1,
             grid=(1,),
             in_specs=[pl.BlockSpec((512, 512), lambda i, sc: (0, 0))] * 4
-            + [whole(a) for a in positions]
+            + [whole(positions)]
             + [pl.BlockSpec(memory_space=pl.ANY)] * 2,
             out_specs=[pl.BlockSpec((CH, 2048), lambda i, sc: (0, 0))] * 2,
             scratch_shapes=[
@@ -398,7 +424,7 @@
         compiler_params=pltpu.CompilerParams(vmem_limit_bytes=VMEM),
         cost_estimate=cost(0.1),
         name="attention_project",
-    )(scalars, *queries, *positions, own, other)
+    )(scalars, *queries, positions, own, other)
 
 
 ORDER = (2, 1, 3)
@@ -468,40 +494,47 @@
     leaving = jnp.take(jnp.concatenate([kept_rows, state_rows], axis=1), picked_slot, axis=0)
     landed = all_to_all(leaving, ("z", "core"))
 
-    place = jnp.stack([2 * (x & 1) + (y & 1), core]).astype(jnp.int32)
+    z = lax.axis_index("z").astype(jnp.int32)
+    place = jnp.stack([2 * (x & 1) + (y & 1), core, z]).astype(jnp.int32)
     *blocks, delta_share = pack(
         after(place, leaving), attn_query, attn_gate, attn_out_weight, delta_out_weight
     )
-    queries = [lax.ppermute(blocks[k], ("x", "y"), regroup(k)) for k in range(4)]
-
-    delta_key = after(delta_key, leaving, *blocks)
+    def regrouped(array, k):
+        return lax.ppermute(array, ("x", "y"), regroup(k))
+
+    def swap_cores(array):
+        return lax.ppermute(array, "core", [(0, 1), (1, 0)])
+
+    delta_own = [delta_share] + [shift(delta_share, "y", d) for d in (1, 2, 3)]
+
+    delta_key = after(delta_key, *blocks)
     prepared = prep(delta_query, delta_key, delta_value, write_strength, decay_log)
-    landed = after(landed, prepared)
+    landed = after(landed, prepared, *delta_own)
+    queries = [regrouped(block, k) for k, block in zip((0, 1), after(blocks[:2], prepared))]
 
     fresh_rows = fresh_kv.transpose(0, 2, 1, 3).reshape(count, 64, 512)
     chosen = select(source, landed, fresh_rows)
     rows = all_to_all(chosen, "x")
-    delta_share = after(delta_share, chosen)
-    delta_own = [delta_share] + [shift(delta_share, "y", d) for d in (1, 2, 3)]
-
-    delta_heads, final_state = scan(after(source, chosen), landed, prepared, delta_gate)
-    attn_own = stack_rows(queries, 1)
-    rows = after(rows, delta_heads, attn_own)
-
-    def swap_cores(array):
-        return lax.ppermute(array, "core", [(0, 1), (1, 0)])
-
+    queries += [regrouped(block, k) for k, block in zip((2, 3), after(blocks[2:], chosen))]
+
+    delta_heads, final_state = scan(after(source, chosen, *queries[:2]), landed, prepared, delta_gate)
+    quarter = [row_of(delta_heads, (y + d) & 3) for d in range(4)]
+    pieces = [quarter[0]] + [shift(quarter[d], "y", d) for d in (1, 2, 3)]
+    rows = after(rows, *queries, *pieces)
+
+    low, high = rows[:, :, :256], rows[:, :, 256:]
+    leaving = jnp.stack([low, high, low, high], axis=0)
+    positions = all_to_all(leaving, "y")
+
+    eighths = stack_rows(after(queries, leaving), CH, 4)
+    eighths = [eighths] + [shift(eighths, "z", d) for d in (1, 2, 3)]
+    delta_own = stack_rows(after(delta_own, leaving), 512, 0)
+    delta_other = swap_cores(delta_own)
+    scalars = jnp.stack([x, core]).astype(jnp.int32)
+    delta_parts = delta_project(scalars, after(pieces, positions), delta_own, delta_other)
+    attn_own = merge_rows(z[None], after(eighths, delta_parts))
     attn_other = swap_cores(attn_own)
-
-    def columns(target):
-        return lax.dynamic_slice_in_dim(rows, (target & 1) * 256, 256, 2)
-
-    parts = [columns(y + d) for d in range(4)]
-    positions = [parts[0]] + [shift(parts[d], "y", d) for d in (1, 2, 3)]
-
-    pieces = all_to_all(after(delta_heads, positions), "y")
-    delta_own = stack_rows(after(delta_own, positions), 0)
-    delta_other = swap_cores(delta_own)
+    positions = after(positions, delta_parts)
 
     def quarters(first, second, *others):
         asked = jnp.stack([x, y, length, (y + first) & 3, (y + second) & 3, core])
@@ -510,9 +543,7 @@
         )
 
     two, one = quarters(2, 1)
-    scalars = jnp.stack([x, y, core]).astype(jnp.int32)
-    delta_parts = delta_project(scalars, after(pieces, two), delta_own, delta_other)
-    three, last = quarters(3, 0, delta_parts)
+    three, last = quarters(3, 0, two)
     delta_mixed = sum_over(delta_parts, "x")
     attn_mixed = sum_over([last, one, two, three], "y")
     return (delta_mixed, attn_mixed, final_state)

time: 197 us -> 189 us (0.959)
  waiting for transfers between devices: 65.3 us -> 51 us
  local copies, waits for them, and re-layouts: 7.79 us -> 11.4 us
  other arithmetic: 8.1 us -> 10.9 us
    ppermute x4, waiting for transfers between devices: 20.1 us -> 0.06 us  [regrouped(): return lax.ppermute(array, ('x', 'y'), regroup(k))]
    all_to_all x3, waiting for transfers between devices: 4.97 us -> 13.3 us  [all_to_all(): return lax.all_to_all(array, axis, split_axis=0, concat_axis=0, tiled=True)]
    all_to_all x3, starting transfers between devices: 14.7 us -> 17.9 us  [all_to_all(): return lax.all_to_all(array, axis, split_axis=0, concat_axis=0, tiled=True)]
    ppermute x4, starting transfers between devices: 14.6 us -> 11.8 us  [regrouped(): return lax.ppermute(array, ('x', 'y'), regroup(k))]
    ppermute x12 -> x15, waiting for transfers between devices: 40.3 us -> 37.7 us  [shift(): return lax.ppermute(array, axis, [(i, (i + by) % 4) for i in range(4)])]
    squeeze x0 -> x1, local copies, waits for them, and re-layouts: none -> 1.99 us  [row_of(): return lax.dynamic_index_in_dim(array, index, 0, keepdims=False)]
    pallas_call x2 -> x3, Pallas kernels: 6.29 us -> 8.04 us  [the longest x2 5.03 us: stack_rows(): pl.pallas_call(stack_kernel, grid=(1,), in_specs=[pl.BlockSpec((rows, 512...]
    ppermute x12 -> x15, starting transfers between devices: 25.9 us -> 26.3 us  [shift(): return lax.ppermute(array, axis, [(i, (i + by) % 4) for i in range(4)])]
  transfers between devices with their start and end apart: 21 -> 24, of which waited for: 9 -> 8; matrix products, arithmetic and copies ran while one was open for 4% -> 6% of each run, Pallas kernels for 26% -> 27%
where the time goes in v2:
time: 189 us; the launch traced here: 188 us
  Pallas kernels  57.6 us (30%)
  starting transfers between devices  56 us (30%)
  waiting for transfers between devices  51 us (27%)
  local copies, waits for them, and re-layouts  11.4 us (6%)
  other arithmetic  10.9 us (6%)
    ppermute x15, waiting for transfers between devices, shift(): return lax.ppermute(array, axis, [(i, (i + by) % 4) for i in range(4)])  37.7 us
    ppermute x15, starting transfers between devices, shift(): return lax.ppermute(array, axis, [(i, (i + by) % 4) for i in range(4)])  26.3 us
    all_to_all x3, starting transfers between devices, all_to_all(): return lax.all_to_all(array, axis, split_axis=0, concat_axis=0, tiled=True)  17.9 us
    pallas_call x2, Pallas kernels, attention(): pl.pallas_call(attention_kernel, grid_spec=pltpu.PrefetchScalarGridSpec(n...  15.8 us
    pallas_call x1, Pallas kernels, prep(): pl.pallas_call(prep_kernel, grid=(chunks,), in_specs=[spec_tok(CH), spec_...  13.6 us
    all_to_all x3, waiting for transfers between devices, all_to_all(): return lax.all_to_all(array, axis, split_axis=0, concat_axis=0, tiled=True)  13.3 us
    ppermute x4, starting transfers between devices, regrouped(): return lax.ppermute(array, ('x', 'y'), regroup(k))  11.8 us
    pallas_call x1, Pallas kernels, scan(): pl.pallas_call(scan_kernel, grid_spec=pltpu.PrefetchScalarGridSpec(num_sc...  7.1 us
  transfers between devices with their start and end apart: 24, of which 8 were waited for; matrix products, arithmetic and copies ran while one was open for 6% of the time, Pallas kernels for 27%

profile of v2, /device:TPU:0, one launch (start us, length us, event | category | flops | bytes accessed | tf_op | source)
XLA Modules:
  0.0 187.8 jit_solution(5662147867724613782)
XLA Ops:
  5.8 5.4 %all-to-all-start = ((bf16[8,192,512]{2,1,0:T(8,128)(2,1)}), bf16[8,192,512]{2,1,0:T(8,128)(2,1)S(1)}, u32[]{:S(2)}, u32[]{:S(2)}) async-start(bf16[8,192,512]{2,1,0:T(8,128)(2,1)} %broadcast_select_fusion), calls=%async_computation | async-start | bytes 3145728 | tf_op jit(solution)/shard_map/all_to_all | solution.py:442
  11.8 4.2 %pack_queries.1 = (bf16[640,512]{1,0:T(8,128)(2,1)}, bf16[640,512]{1,0:T(8,128)(2,1)}, bf16[640,512]{1,0:T(8,128)(2,1)}, bf16[640,512]{1,0:T(8,128)(2,1)}, bf16[512,512]{1,0:T(8,128)(2,1)}) custom-call(s32[3]{0:T(128)} %pad_add_fusion.1.sc_ref, bf16[4,512,256]{2,1,0:T(8,128)(2,1)} %q_ref.2, bf16[4,512,256]{2,1,0:T(8,128)(2,1)} %g_ref.2, ...), custom_call_target="tpu_custom_call" | custom-call | flops 100000000 | bytes 300000 | tf_op jit(solution)/shard_map/pack_queries/pallas_call | solution.py:251
  17.5 2.9 %collective-permute-start.1 = (bf16[512,512]{1,0:T(8,128)(2,1)}, bf16[512,512]{1,0:T(8,128)(2,1)}, u32[]{:S(2)}, u32[]{:S(2)}) collective-permute-start(bf16[512,512]{1,0:T(8,128)(2,1)} %get-tuple-element.74.r0), channel_id=1, source_target_pairs={{0,2},{1,3},{2,0},{3,1},{4,6},{5,7},{6,4},{7,5},{8,10},{9,11},{10,... | collective-permute-start | bytes 1572872 | tf_op jit(solution)/shard_map/ppermute | solution.py:434
  21.7 13.6 %delta_prep.1 = (bf16[4,8,256,128]{3,2,1,0:T(8,128)(2,1)}, f32[4,8,128,128]{3,2,1,0:T(8,128)}, bf16[4,8,128,128]{3,2,1,0:T(8,128)(2,1)}, bf16[4,8,128,128]{3,2,1,0:T(8,128)(2,1)}, f32[4,8,128]{2,1,0:T(8,128)}) custom-call(bf16[4,512,128]{2,1,0:T(8,128)(2,1)} %q_ref.3, bf16[4,512,128]{2,1,0:T(8,128)(2,1)} %k_ref, bf16[4,512,256]{2,1,0:T(8,128)(2,1)} %v_ref.1, ...), custom_call_target="tpu_custom_call" | custom-call | flops 100000000 | bytes 300000 | tf_op jit(solution)/shard_map/delta_prep/pallas_call | solution.py:110
  37.1 5.1 %collective-permute-start.4 = (bf16[640,512]{1,0:T(8,128)(2,1)}, bf16[640,512]{1,0:T(8,128)(2,1)S(1)}, u32[]{:S(2)}, u32[]{:S(2)}) collective-permute-start(bf16[640,512]{1,0:T(8,128)(2,1)} %get-tuple-element.64), channel_id=1, source_target_pairs={{0,4},{1,8},{2,6},{3,10},{4,12},{5,0},{6,14},{7,2},{8,5},{9,9},{10... | collective-permute-start | bytes 1966088 | tf_op jit(solution)/shard_map/ppermute | solution.py:503
  44.6 13.7 %collective-permute-done.1.r2 = bf16[512,512]{1,0:T(8,128)(2,1)} collective-permute-done((bf16[512,512]{1,0:T(8,128)(2,1)}, bf16[512,512]{1,0:T(8,128)(2,1)}, u32[]{:S(2)}, u32[]{:S(2)}) %collective-permute-start.1) | collective-permute-done | bytes 524320 | tf_op jit(solution)/shard_map/ppermute | solution.py:434
  59.5 2.4 %select_sessions.1 = bf16[4,192,512]{2,1,0:T(8,128)(2,1)} custom-call(s32[4]{0:T(128)} %and_select_fusion.2.src_ref, bf16[8,192,512]{2,1,0:T(8,128)(2,1)} %copy-done.1, bf16[4,64,512]{2,1,0:T(8,128)(2,1)} %bitcast.37), custom_call_target="tpu_custom_call" | custom-call | flops 100000000 | bytes 300000 | tf_op jit(solution)/shard_map/select_sessions/pallas_call | solution.py:321
  61.9 3.0 %collective-permute-start.8 = (bf16[640,512]{1,0:T(8,128)(2,1)}, bf16[640,512]{1,0:T(8,128)(2,1)S(1)}, u32[]{:S(2)}, u32[]{:S(2)}) collective-permute-start(bf16[640,512]{1,0:T(8,128)(2,1)} %get-tuple-element.67), channel_id=1, source_target_pairs={{0,8},{1,12},{2,10},{3,14},{4,0},{5,4},{6,2},{7,6},{8,9},{9,13},{1... | collective-permute-start | bytes 1966088 | tf_op jit(solution)/shard_map/ppermute | solution.py:503
  66.9 3.5 %all-to-all-start.1 = ((bf16[4,192,512]{2,1,0:T(8,128)(2,1)}), bf16[4,192,512]{2,1,0:T(8,128)(2,1)S(1)}, u32[]{:S(2)}, u32[]{:S(2)}) async-start(bf16[4,192,512]{2,1,0:T(8,128)(2,1)} %select_sessions.1), calls=%async_computation.1 | async-start | bytes 1572864 | tf_op jit(solution)/shard_map/all_to_all | solution.py:442
  70.5 7.1 %delta_scan.1 = (bf16[4,4,128,256]{3,2,1,0:T(8,128)(2,1)}, f32[4,2,128,128]{3,2,1,0:T(8,128)}) custom-call(s32[4]{0:T(128)} %and_select_fusion.2.src_ref, bf16[8,192,512]{2,1,0:T(8,128)(2,1)} %copy-done.1, bf16[4,8,256,128]{3,2,1,0:T(8,128)(2,1)} %get-tuple-element.56.wq_ref, f32[4,8,128,128]{3,2,1,0:T(8,128)} %get-tuple-element.57.u_ref, ...), custom_call_target="tpu_custom_call" | custom-call | flops 100000000 | bytes 300000 | tf_op jit(solution)/shard_map/delta_scan/pallas_call | solution.py:171
  81.5 3.0 %collective-permute-start.6 = (bf16[4,128,256]{2,1,0:T(8,128)(2,1)S(1)}, bf16[4,128,256]{2,1,0:T(8,128)(2,1)S(1)}, u32[]{:S(2)}, u32[]{:S(2)}) collective-permute-start(bf16[4,128,256]{2,1,0:T(8,128)(2,1)S(1)} %get-tuple-element.98), channel_id=1, source_target_pairs={{0,2},{1,3},{2,0},{3,1},{4,6},{5,7},{6,4},{7,5},{8,10},{9,11},{10,... | collective-permute-start | bytes 786440 | tf_op jit(solution)/shard_map/ppermute | solution.py:434
  85.1 4.9 %collective-permute-done.5.h1 = bf16[4,128,256]{2,1,0:T(8,128)(2,1)S(1)} collective-permute-done((bf16[4,128,256]{2,1,0:T(8,128)(2,1)S(1)}, bf16[4,128,256]{2,1,0:T(8,128)(2,1)S(1)}, u32[]{:S(2)}, u32[]{:S(2)}) %collective-permute-start.5) | collective-permute-done | bytes 262176 | tf_op jit(solution)/shard_map/ppermute | solution.py:434
  90.0 5.0 %collective-permute-done.6.h2 = bf16[4,128,256]{2,1,0:T(8,128)(2,1)S(1)} collective-permute-done((bf16[4,128,256]{2,1,0:T(8,128)(2,1)S(1)}, bf16[4,128,256]{2,1,0:T(8,128)(2,1)S(1)}, u32[]{:S(2)}, u32[]{:S(2)}) %collective-permute-start.6) | collective-permute-done | bytes 262176 | tf_op jit(solution)/shard_map/ppermute | solution.py:434
  97.4 3.0 %stack_weights.2.own_ref = bf16[4,512,512]{2,1,0:T(8,128)(2,1)} custom-call(bf16[512,512]{1,0:T(8,128)(2,1)} %get-tuple-element.74.r0, bf16[512,512]{1,0:T(8,128)(2,1)} %copy-done.13, bf16[512,512]{1,0:T(8,128)(2,1)} %collective-permute-done.1.r2, bf16[512,512]{1,0:T(8,128)(2,1)} %collective-permute-done.2.r3), custom_call_target="tpu_custom_call" | custom-call | flops 100000000 | bytes 300000 | tf_op jit(solution)/shard_map/stack_weights/pallas_call | solution.py:279
  100.4 9.0 %all-to-all-start.2 = ((bf16[4,4,192,256]{3,2,1,0:T(8,128)(2,1)}), bf16[4,4,192,256]{3,2,1,0:T(8,128)(2,1)S(1)}, u32[]{:S(2)}, u32[]{:S(2)}) async-start(bf16[4,4,192,256]{3,2,1,0:T(8,128)(2,1)} %pad_maximum_fusion), calls=%async_computation.2 | async-start | bytes 3145728 | tf_op jit(solution)/shard_map/all_to_all | solution.py:442
  112.8 2.7 %collective-permute-start.15 = (bf16[4,128,512]{2,1,0:T(8,128)(2,1)}, bf16[4,128,512]{2,1,0:T(8,128)(2,1)S(1)}, u32[]{:S(2)}, u32[]{:S(2)}) collective-permute-start(bf16[4,128,512]{2,1,0:T(8,128)(2,1)} %stack_weights.3.r0), channel_id=1, source_target_pairs={{0,64},{32,96},{64,0},{96,32},{1,65},{33,97},{65,1},{97,33},{2,66}... | collective-permute-start | bytes 1572872 | tf_op jit(solution)/shard_map/ppermute | solution.py:434
  117.6 13.3 %all-to-all-done.2.place_ref = bf16[4,4,192,256]{3,2,1,0:T(8,128)(2,1)S(1)} async-done(((bf16[4,4,192,256]{3,2,1,0:T(8,128)(2,1)}), bf16[4,4,192,256]{3,2,1,0:T(8,128)(2,1)S(1)}, u32[]{:S(2)}, u32[]{:S(2)}) %all-to-all-start.2) | async-done | bytes 1572896 | tf_op jit(solution)/shard_map/all_to_all | solution.py:442
  130.8 6.5 %delta_project.1 = (bf16[128,2048]{1,0:T(8,128)(2,1)}, bf16[128,2048]{1,0:T(8,128)(2,1)}, bf16[128,2048]{1,0:T(8,128)(2,1)}, bf16[128,2048]{1,0:T(8,128)(2,1)}) custom-call(s32[2]{0:T(128)} %pad_add_fusion.sc_ref, bf16[4,128,256]{2,1,0:T(8,128)(2,1)} %get-tuple-element.70.h0, bf16[4,128,256]{2,1,0:T(8,128)(2,1)} %copy-done.14, ...), custom_call_target="tpu_custom_call" | custom-call | flops 100000000 | bytes 300000 | tf_op jit(solution)/shard_map/delta_project/pallas_call | solution.py:223
  139.9 3.0 %merge_weights.1.own_hbm = bf16[4,512,512]{2,1,0:T(8,128)(2,1)} custom-call(s32[1]{0:T(128)} %bitcast.9.sc_ref, bf16[4,128,512]{2,1,0:T(8,128)(2,1)} %stack_weights.3.r0, bf16[4,128,512]{2,1,0:T(8,128)(2,1)} %copy-done.9, bf16[4,128,512]{2,1,0:T(8,128)(2,1)} %copy-done.10, bf16[4,128,512]{2,1,0:T(8,128)(2,1)} %copy-done.11), custom_call_target="tpu_custom_call" | custom-call | flops 100000000 | bytes 300000 | tf_op jit(solution)/shard_map/merge_weights/pallas_call | solution.py:302
  143.8 3.2 %collective-permute-start.13 = (bf16[128,2048]{1,0:T(8,128)(2,1)}, bf16[128,2048]{1,0:T(8,128)(2,1)}, u32[]{:S(2)}, u32[]{:S(2)}) collective-permute-start(bf16[128,2048]{1,0:T(8,128)(2,1)} %get-tuple-element.81), channel_id=1, source_target_pairs={{0,12},{4,0},{8,4},{12,8},{1,13},{5,1},{9,5},{13,9},{2,14},{6,2},{... | collective-permute-start | bytes 1572872 | tf_op jit(solution)/shard_map/ppermute | solution.py:434
  151.5 7.9 %attention_project.2 = (bf16[128,2048]{1,0:T(8,128)(2,1)}, bf16[128,2048]{1,0:T(8,128)(2,1)}) custom-call(s32[6]{0:T(128)} %stack.73.sc_ref, bf16[640,512]{1,0:T(8,128)(2,1)} %copy-done.3, bf16[640,512]{1,0:T(8,128)(2,1)} %copy-done.4, bf16[640,512]{1,0:T(8,128)(2,1)} %copy-done.5, bf16[640,512]{1,0:T(8,128)(2,1)} %copy-done.6, ...), custom_call_target="tpu_custom_call" | custom-call | flops 100000000 | bytes 300000 | tf_op jit(solution)/shard_map/attention_project/pallas_call | solution.py:406
  159.4 3.3 %collective-permute-start.18 = (bf16[128,2048]{1,0:T(8,128)(2,1)}, bf16[128,2048]{1,0:T(8,128)(2,1)S(1)}, u32[]{:S(2)}, u32[]{:S(2)}) collective-permute-start(bf16[128,2048]{1,0:T(8,128)(2,1)} %get-tuple-element.91), channel_id=1, source_target_pairs={{0,2},{1,3},{2,0},{3,1},{4,6},{5,7},{6,4},{7,5},{8,10},{9,11},{10,... | collective-permute-start | bytes 1572872 | tf_op jit(solution)/shard_map/ppermute | solution.py:434
  162.7 7.8 %attention_project.3 = (bf16[128,2048]{1,0:T(8,128)(2,1)}, bf16[128,2048]{1,0:T(8,128)(2,1)}) custom-call(s32[6]{0:T(128)} %stack.70.sc_ref, bf16[640,512]{1,0:T(8,128)(2,1)} %copy-done.3, bf16[640,512]{1,0:T(8,128)(2,1)} %copy-done.4, bf16[640,512]{1,0:T(8,128)(2,1)} %copy-done.5, bf16[640,512]{1,0:T(8,128)(2,1)} %copy-done.6, ...), custom_call_target="tpu_custom_call" | custom-call | flops 100000000 | bytes 300000 | tf_op jit(solution)/shard_map/attention_project/pallas_call | solution.py:406
  174.9 11.4 %collective-permute-done.20 = bf16[128,2048]{1,0:T(8,128)(2,1)S(1)} collective-permute-done((bf16[128,2048]{1,0:T(8,128)(2,1)}, bf16[128,2048]{1,0:T(8,128)(2,1)S(1)}, u32[]{:S(2)}, u32[]{:S(2)}) %collective-permute-start.20) | collective-permute-done | bytes 524320 | tf_op jit(solution)/shard_map/ppermute | solution.py:434
  (97 shorter events, 41.9 us)
Async XLA Ops:
  5.8 52.5 %all-to-all-start = ((bf16[8,192,512]{2,1,0:T(8,128)(2,1)}), bf16[8,192,512]{2,1,0:T(8,128)(2,1)S(1)}, u32[]{:S(2)}, u32[]{:S(2)}) async-start(bf16[8,192,512]{2,1,0:T(8,128)(2,1)} %broadcast_select_fusion), calls=%async_computation | async-start | bytes 3145728 | tf_op jit(solution)/shard_map/all_to_all | solution.py:442
  15.9 28.7 %collective-permute-start = (bf16[512,512]{1,0:T(8,128)(2,1)}, bf16[512,512]{1,0:T(8,128)(2,1)S(1)}, u32[]{:S(2)}, u32[]{:S(2)}) collective-permute-start(bf16[512,512]{1,0:T(8,128)(2,1)} %get-tuple-element.74.r0), channel_id=1, source_target_pairs={{0,1},{1,2},{2,3},{3,0},{4,5},{5,6},{6,7},{7,4},{8,9},{9,10},{10,1... | collective-permute-start | bytes 1572872 | tf_op jit(solution)/shard_map/ppermute | solution.py:434
  17.5 40.8 %collective-permute-start.1 = (bf16[512,512]{1,0:T(8,128)(2,1)}, bf16[512,512]{1,0:T(8,128)(2,1)}, u32[]{:S(2)}, u32[]{:S(2)}) collective-permute-start(bf16[512,512]{1,0:T(8,128)(2,1)} %get-tuple-element.74.r0), channel_id=1, source_target_pairs={{0,2},{1,3},{2,0},{3,1},{4,6},{5,7},{6,4},{7,5},{8,10},{9,11},{10,... | collective-permute-start | bytes 1572872 | tf_op jit(solution)/shard_map/ppermute | solution.py:434
  20.4 37.9 %collective-permute-start.2 = (bf16[512,512]{1,0:T(8,128)(2,1)}, bf16[512,512]{1,0:T(8,128)(2,1)}, u32[]{:S(2)}, u32[]{:S(2)}) collective-permute-start(bf16[512,512]{1,0:T(8,128)(2,1)} %get-tuple-element.74.r0), channel_id=1, source_target_pairs={{0,3},{1,0},{2,1},{3,2},{4,7},{5,4},{6,5},{7,6},{8,11},{9,8},{10,9... | collective-permute-start | bytes 1572872 | tf_op jit(solution)/shard_map/ppermute | solution.py:434
  35.4 35.0 %collective-permute-start.3 = (bf16[640,512]{1,0:T(8,128)(2,1)}, bf16[640,512]{1,0:T(8,128)(2,1)S(1)}, u32[]{:S(2)}, u32[]{:S(2)}) collective-permute-start(bf16[640,512]{1,0:T(8,128)(2,1)} %get-tuple-element.63), channel_id=1, source_target_pairs={{0,0},{1,4},{2,2},{3,6},{4,8},{5,12},{6,10},{7,14},{8,1},{9,5},{10... | collective-permute-start | bytes 1966088 | tf_op jit(solution)/shard_map/ppermute | solution.py:503
  37.1 33.3 %collective-permute-start.4 = (bf16[640,512]{1,0:T(8,128)(2,1)}, bf16[640,512]{1,0:T(8,128)(2,1)S(1)}, u32[]{:S(2)}, u32[]{:S(2)}) collective-permute-start(bf16[640,512]{1,0:T(8,128)(2,1)} %get-tuple-element.64), channel_id=1, source_target_pairs={{0,4},{1,8},{2,6},{3,10},{4,12},{5,0},{6,14},{7,2},{8,5},{9,9},{10... | collective-permute-start | bytes 1966088 | tf_op jit(solution)/shard_map/ppermute | solution.py:503
  61.9 33.8 %collective-permute-start.8 = (bf16[640,512]{1,0:T(8,128)(2,1)}, bf16[640,512]{1,0:T(8,128)(2,1)S(1)}, u32[]{:S(2)}, u32[]{:S(2)}) collective-permute-start(bf16[640,512]{1,0:T(8,128)(2,1)} %get-tuple-element.67), channel_id=1, source_target_pairs={{0,8},{1,12},{2,10},{3,14},{4,0},{5,4},{6,2},{7,6},{8,9},{9,13},{1... | collective-permute-start | bytes 1966088 | tf_op jit(solution)/shard_map/ppermute | solution.py:503
  64.9 30.8 %collective-permute-start.9 = (bf16[640,512]{1,0:T(8,128)(2,1)}, bf16[640,512]{1,0:T(8,128)(2,1)S(1)}, u32[]{:S(2)}, u32[]{:S(2)}) collective-permute-start(bf16[640,512]{1,0:T(8,128)(2,1)} %get-tuple-element.68), channel_id=1, source_target_pairs={{0,12},{1,0},{2,14},{3,2},{4,4},{5,8},{6,6},{7,10},{8,13},{9,1},{1... | collective-permute-start | bytes 1966088 | tf_op jit(solution)/shard_map/ppermute | solution.py:503
  66.9 28.8 %all-to-all-start.1 = ((bf16[4,192,512]{2,1,0:T(8,128)(2,1)}), bf16[4,192,512]{2,1,0:T(8,128)(2,1)S(1)}, u32[]{:S(2)}, u32[]{:S(2)}) async-start(bf16[4,192,512]{2,1,0:T(8,128)(2,1)} %select_sessions.1), calls=%async_computation.1 | async-start | bytes 1572864 | tf_op jit(solution)/shard_map/all_to_all | solution.py:442
  79.6 10.4 %collective-permute-start.5 = (bf16[4,128,256]{2,1,0:T(8,128)(2,1)S(1)}, bf16[4,128,256]{2,1,0:T(8,128)(2,1)S(1)}, u32[]{:S(2)}, u32[]{:S(2)}) collective-permute-start(bf16[4,128,256]{2,1,0:T(8,128)(2,1)S(1)} %get-tuple-element.99), channel_id=1, source_target_pairs={{0,1},{1,2},{2,3},{3,0},{4,5},{5,6},{6,7},{7,4},{8,9},{9,10},{10,1... | collective-permute-start | bytes 786440 | tf_op jit(solution)/shard_map/ppermute | solution.py:434
  81.5 13.4 %collective-permute-start.6 = (bf16[4,128,256]{2,1,0:T(8,128)(2,1)S(1)}, bf16[4,128,256]{2,1,0:T(8,128)(2,1)S(1)}, u32[]{:S(2)}, u32[]{:S(2)}) collective-permute-start(bf16[4,128,256]{2,1,0:T(8,128)(2,1)S(1)} %get-tuple-element.98), channel_id=1, source_target_pairs={{0,2},{1,3},{2,0},{3,1},{4,6},{5,7},{6,4},{7,5},{8,10},{9,11},{10,... | collective-permute-start | bytes 786440 | tf_op jit(solution)/shard_map/ppermute | solution.py:434
  84.6 11.1 %collective-permute-start.7 = (bf16[4,128,256]{2,1,0:T(8,128)(2,1)S(1)}, bf16[4,128,256]{2,1,0:T(8,128)(2,1)S(1)}, u32[]{:S(2)}, u32[]{:S(2)}) collective-permute-start(bf16[4,128,256]{2,1,0:T(8,128)(2,1)S(1)} %get-tuple-element.97), channel_id=1, source_target_pairs={{0,3},{1,0},{2,1},{3,2},{4,7},{5,4},{6,5},{7,6},{8,11},{9,8},{10,9... | collective-permute-start | bytes 786440 | tf_op jit(solution)/shard_map/ppermute | solution.py:434
  100.4 30.4 %collective-permute-start.10 = (bf16[4,512,512]{2,1,0:T(8,128)(2,1)}, bf16[4,512,512]{2,1,0:T(8,128)(2,1)}, u32[]{:S(2)}, u32[]{:S(2)}) collective-permute-start(bf16[4,512,512]{2,1,0:T(8,128)(2,1)} %stack_weights.2.own_ref), channel_id=1, source_target_pairs={{0,16},{16,0},{1,17},{17,1},{2,18},{18,2},{3,19},{19,3},{4,20},{20... | collective-permute-start | bytes 6291464 | tf_op jit(solution)/shard_map/ppermute | solution.py:506
  100.4 30.4 %all-to-all-start.2 = ((bf16[4,4,192,256]{3,2,1,0:T(8,128)(2,1)}), bf16[4,4,192,256]{3,2,1,0:T(8,128)(2,1)S(1)}, u32[]{:S(2)}, u32[]{:S(2)}) async-start(bf16[4,4,192,256]{3,2,1,0:T(8,128)(2,1)} %pad_maximum_fusion), calls=%async_computation.2 | async-start | bytes 3145728 | tf_op jit(solution)/shard_map/all_to_all | solution.py:442
  111.4 25.9 %collective-permute-start.14 = (bf16[4,128,512]{2,1,0:T(8,128)(2,1)}, bf16[4,128,512]{2,1,0:T(8,128)(2,1)S(1)}, u32[]{:S(2)}, u32[]{:S(2)}) collective-permute-start(bf16[4,128,512]{2,1,0:T(8,128)(2,1)} %stack_weights.3.r0), channel_id=1, source_target_pairs={{0,32},{32,64},{64,96},{96,0},{1,33},{33,65},{65,97},{97,1},{2,34}... | collective-permute-start | bytes 1572872 | tf_op jit(solution)/shard_map/ppermute | solution.py:434
  112.8 26.2 %collective-permute-start.15 = (bf16[4,128,512]{2,1,0:T(8,128)(2,1)}, bf16[4,128,512]{2,1,0:T(8,128)(2,1)S(1)}, u32[]{:S(2)}, u32[]{:S(2)}) collective-permute-start(bf16[4,128,512]{2,1,0:T(8,128)(2,1)} %stack_weights.3.r0), channel_id=1, source_target_pairs={{0,64},{32,96},{64,0},{96,32},{1,65},{33,97},{65,1},{97,33},{2,66}... | collective-permute-start | bytes 1572872 | tf_op jit(solution)/shard_map/ppermute | solution.py:434
  115.5 23.5 %collective-permute-start.16 = (bf16[4,128,512]{2,1,0:T(8,128)(2,1)}, bf16[4,128,512]{2,1,0:T(8,128)(2,1)S(1)}, u32[]{:S(2)}, u32[]{:S(2)}) collective-permute-start(bf16[4,128,512]{2,1,0:T(8,128)(2,1)} %stack_weights.3.r0), channel_id=1, source_target_pairs={{0,96},{32,0},{64,32},{96,64},{1,97},{33,1},{65,33},{97,65},{2,98}... | collective-permute-start | bytes 1572872 | tf_op jit(solution)/shard_map/ppermute | solution.py:434
  142.9 7.3 %collective-permute-start.17 = (bf16[4,512,512]{2,1,0:T(8,128)(2,1)}, bf16[4,512,512]{2,1,0:T(8,128)(2,1)S(1)}, u32[]{:S(2)}, u32[]{:S(2)}) collective-permute-start(bf16[4,512,512]{2,1,0:T(8,128)(2,1)} %merge_weights.1.own_hbm), channel_id=1, source_target_pairs={{0,16},{16,0},{1,17},{17,1},{2,18},{18,2},{3,19},{19,3},{4,20},{20... | collective-permute-start | bytes 6291464 | tf_op jit(solution)/shard_map/ppermute | solution.py:506
  142.9 28.9 %collective-permute-start.11 = (bf16[128,2048]{1,0:T(8,128)(2,1)}, bf16[128,2048]{1,0:T(8,128)(2,1)S(1)}, u32[]{:S(2)}, u32[]{:S(2)}) collective-permute-start(bf16[128,2048]{1,0:T(8,128)(2,1)} %get-tuple-element.79), channel_id=1, source_target_pairs={{0,8},{4,12},{8,0},{12,4},{1,9},{5,13},{9,1},{13,5},{2,10},{6,14},... | collective-permute-start | bytes 1572872 | tf_op jit(solution)/shard_map/ppermute | solution.py:434
  143.8 28.9 %collective-permute-start.12 = (bf16[128,2048]{1,0:T(8,128)(2,1)}, bf16[128,2048]{1,0:T(8,128)(2,1)S(1)}, u32[]{:S(2)}, u32[]{:S(2)}) collective-permute-start(bf16[128,2048]{1,0:T(8,128)(2,1)} %get-tuple-element.80), channel_id=1, source_target_pairs={{0,4},{4,8},{8,12},{12,0},{1,5},{5,9},{9,13},{13,1},{2,6},{6,10},{... | collective-permute-start | bytes 1572872 | tf_op jit(solution)/shard_map/ppermute | solution.py:434
  143.8 28.9 %collective-permute-start.13 = (bf16[128,2048]{1,0:T(8,128)(2,1)}, bf16[128,2048]{1,0:T(8,128)(2,1)}, u32[]{:S(2)}, u32[]{:S(2)}) collective-permute-start(bf16[128,2048]{1,0:T(8,128)(2,1)} %get-tuple-element.81), channel_id=1, source_target_pairs={{0,12},{4,0},{8,4},{12,8},{1,13},{5,1},{9,5},{13,9},{2,14},{6,2},{... | collective-permute-start | bytes 1572872 | tf_op jit(solution)/shard_map/ppermute | solution.py:434
  159.4 26.8 %collective-permute-start.18 = (bf16[128,2048]{1,0:T(8,128)(2,1)}, bf16[128,2048]{1,0:T(8,128)(2,1)S(1)}, u32[]{:S(2)}, u32[]{:S(2)}) collective-permute-start(bf16[128,2048]{1,0:T(8,128)(2,1)} %get-tuple-element.91), channel_id=1, source_target_pairs={{0,2},{1,3},{2,0},{3,1},{4,6},{5,7},{6,4},{7,5},{8,10},{9,11},{10,... | collective-permute-start | bytes 1572872 | tf_op jit(solution)/shard_map/ppermute | solution.py:434
  170.6 15.6 %collective-permute-start.20 = (bf16[128,2048]{1,0:T(8,128)(2,1)}, bf16[128,2048]{1,0:T(8,128)(2,1)S(1)}, u32[]{:S(2)}, u32[]{:S(2)}) collective-permute-start(bf16[128,2048]{1,0:T(8,128)(2,1)} %get-tuple-element.95), channel_id=1, source_target_pairs={{0,3},{1,0},{2,1},{3,2},{4,7},{5,4},{6,5},{7,6},{8,11},{9,8},{10,9... | collective-permute-start | bytes 1572872 | tf_op jit(solution)/shard_map/ppermute | solution.py:434
  171.8 14.8 %collective-permute-start.19 = (bf16[128,2048]{1,0:T(8,128)(2,1)}, bf16[128,2048]{1,0:T(8,128)(2,1)S(1)}, u32[]{:S(2)}, u32[]{:S(2)}) collective-permute-start(bf16[128,2048]{1,0:T(8,128)(2,1)} %get-tuple-element.94), channel_id=1, source_target_pairs={{0,1},{1,2},{2,3},{3,0},{4,5},{5,6},{6,7},{7,4},{8,9},{9,10},{10,1... | collective-permute-start | bytes 1572872 | tf_op jit(solution)/shard_map/ppermute | solution.py:434
  (19 other events, 131.2 us)

commit v3 on v2

--- a/solution.py
+++ b/solution.py
@@ -505,22 +505,21 @@
     def swap_cores(array):
         return lax.ppermute(array, "core", [(0, 1), (1, 0)])
 
-    delta_own = [delta_share] + [shift(delta_share, "y", d) for d in (1, 2, 3)]
-
-    delta_key = after(delta_key, *blocks)
-    prepared = prep(delta_query, delta_key, delta_value, write_strength, decay_log)
-    landed = after(landed, prepared, *delta_own)
-    queries = [regrouped(block, k) for k, block in zip((0, 1), after(blocks[:2], prepared))]
+    queries = [regrouped(blocks[k], k) for k in range(4)]
 
     fresh_rows = fresh_kv.transpose(0, 2, 1, 3).reshape(count, 64, 512)
+    landed = after(landed, *blocks)
     chosen = select(source, landed, fresh_rows)
     rows = all_to_all(chosen, "x")
-    queries += [regrouped(block, k) for k, block in zip((2, 3), after(blocks[2:], chosen))]
-
-    delta_heads, final_state = scan(after(source, chosen, *queries[:2]), landed, prepared, delta_gate)
+    delta_share = after(delta_share, chosen)
+    delta_own = [delta_share] + [shift(delta_share, "y", d) for d in (1, 2, 3)]
+
+    delta_key = after(delta_key, chosen)
+    prepared = prep(delta_query, delta_key, delta_value, write_strength, decay_log)
+    delta_heads, final_state = scan(source, landed, prepared, delta_gate)
     quarter = [row_of(delta_heads, (y + d) & 3) for d in range(4)]
     pieces = [quarter[0]] + [shift(quarter[d], "y", d) for d in (1, 2, 3)]
-    rows = after(rows, *queries, *pieces)
+    rows = after(rows, delta_heads, *queries)
 
     low, high = rows[:, :, :256], rows[:, :, 256:]
     leaving = jnp.stack([low, high, low, high], axis=0)
@@ -528,13 +527,11 @@
 
     eighths = stack_rows(after(queries, leaving), CH, 4)
     eighths = [eighths] + [shift(eighths, "z", d) for d in (1, 2, 3)]
-    delta_own = stack_rows(after(delta_own, leaving), 512, 0)
+    delta_own = stack_rows(after(delta_own, positions), 512, 0)
     delta_other = swap_cores(delta_own)
     scalars = jnp.stack([x, core]).astype(jnp.int32)
-    delta_parts = delta_project(scalars, after(pieces, positions), delta_own, delta_other)
-    attn_own = merge_rows(z[None], after(eighths, delta_parts))
+    attn_own = merge_rows(z[None], after(eighths, positions))
     attn_other = swap_cores(attn_own)
-    positions = after(positions, delta_parts)
 
     def quarters(first, second, *others):
         asked = jnp.stack([x, y, length, (y + first) & 3, (y + second) & 3, core])
@@ -543,7 +540,8 @@
         )
 
     two, one = quarters(2, 1)
-    three, last = quarters(3, 0, two)
+    delta_parts = delta_project(scalars, after(pieces, two), delta_own, delta_other)
+    three, last = quarters(3, 0, delta_parts)
     delta_mixed = sum_over(delta_parts, "x")
     attn_mixed = sum_over([last, one, two, three], "y")
     return (delta_mixed, attn_mixed, final_state)

time: 189 us -> 179 us (0.947)
  waiting for transfers between devices: 51 us -> 41.3 us
    all_to_all x3, waiting for transfers between devices: 13.3 us -> 0.01 us  [all_to_all(): return lax.all_to_all(array, axis, split_axis=0, concat_axis=0, tiled=True)]
    ppermute x15, waiting for transfers between devices: 37.7 us -> 41.3 us  [shift(): return lax.ppermute(array, axis, [(i, (i + by) % 4) for i in range(4)])]
    ppermute x4, starting transfers between devices: 11.8 us -> 14.5 us  [regrouped(): return lax.ppermute(array, ('x', 'y'), regroup(k))]
    all_to_all x3, starting transfers between devices: 17.9 us -> 15.6 us  [all_to_all(): return lax.all_to_all(array, axis, split_axis=0, concat_axis=0, tiled=True)]
  transfers between devices with their start and end apart: 24 -> 24, of which waited for: 8 -> 6; matrix products, arithmetic and copies ran while one was open for 6% -> 5% of each run, Pallas kernels for 27% -> 29%
where the time goes in v3:
time: 179 us; the launch traced here: 177 us
  Pallas kernels  58.3 us (33%)
  starting transfers between devices  55.6 us (31%)
  waiting for transfers between devices  41.3 us (23%)
  local copies, waits for them, and re-layouts  11 us (6%)
  other arithmetic  9.84 us (5%)
    ppermute x15, waiting for transfers between devices, shift(): return lax.ppermute(array, axis, [(i, (i + by) % 4) for i in range(4)])  41.3 us
    ppermute x15, starting transfers between devices, shift(): return lax.ppermute(array, axis, [(i, (i + by) % 4) for i in range(4)])  25.4 us
    pallas_call x2, Pallas kernels, attention(): pl.pallas_call(attention_kernel, grid_spec=pltpu.PrefetchScalarGridSpec(n...  15.8 us
    all_to_all x3, starting transfers between devices, all_to_all(): return lax.all_to_all(array, axis, split_axis=0, concat_axis=0, tiled=True)  15.6 us
    ppermute x4, starting transfers between devices, regrouped(): return lax.ppermute(array, ('x', 'y'), regroup(k))  14.5 us
    pallas_call x1, Pallas kernels, prep(): pl.pallas_call(prep_kernel, grid=(chunks,), in_specs=[spec_tok(CH), spec_...  13.7 us
    pallas_call x1, Pallas kernels, scan(): pl.pallas_call(scan_kernel, grid_spec=pltpu.PrefetchScalarGridSpec(num_sc...  7.13 us
    pallas_call x1, Pallas kernels, delta_project(): pl.pallas_call(delta_project_kernel, grid_spec=pltpu.PrefetchScalarGridSp...  6.51 us
  transfers between devices with their start and end apart: 24, of which 6 were waited for; matrix products, arithmetic and copies ran while one was open for 5% of the time, Pallas kernels for 29%

profile of v3, /device:TPU:0, one launch (start us, length us, event | category | flops | bytes accessed | tf_op | source)
XLA Modules:
  0.0 177.0 jit_solution(6877887649364882267)
XLA Ops:
  5.7 5.4 %all-to-all-start = ((bf16[8,192,512]{2,1,0:T(8,128)(2,1)}), bf16[8,192,512]{2,1,0:T(8,128)(2,1)S(1)}, u32[]{:S(2)}, u32[]{:S(2)}) async-start(bf16[8,192,512]{2,1,0:T(8,128)(2,1)} %broadcast_select_fusion), calls=%async_computation | async-start | bytes 3145728 | tf_op jit(solution)/shard_map/all_to_all | solution.py:442
  11.7 4.3 %pack_queries.1 = (bf16[640,512]{1,0:T(8,128)(2,1)}, bf16[640,512]{1,0:T(8,128)(2,1)}, bf16[640,512]{1,0:T(8,128)(2,1)}, bf16[640,512]{1,0:T(8,128)(2,1)}, bf16[512,512]{1,0:T(8,128)(2,1)}) custom-call(s32[3]{0:T(128)} %pad_add_fusion.1.sc_ref, bf16[4,512,256]{2,1,0:T(8,128)(2,1)} %q_ref.2, bf16[4,512,256]{2,1,0:T(8,128)(2,1)} %g_ref.2, ...), custom_call_target="tpu_custom_call" | custom-call | flops 100000000 | bytes 300000 | tf_op jit(solution)/shard_map/pack_queries/pallas_call | solution.py:251
  17.7 5.1 %collective-permute-start.4 = (bf16[640,512]{1,0:T(8,128)(2,1)}, bf16[640,512]{1,0:T(8,128)(2,1)S(1)}, u32[]{:S(2)}, u32[]{:S(2)}) collective-permute-start(bf16[640,512]{1,0:T(8,128)(2,1)} %get-tuple-element.47), channel_id=1, source_target_pairs={{0,4},{1,8},{2,6},{3,10},{4,12},{5,0},{6,14},{7,2},{8,5},{9,9},{10... | collective-permute-start | bytes 1966088 | tf_op jit(solution)/shard_map/ppermute | solution.py:503
  22.8 3.7 %collective-permute-start.5 = (bf16[640,512]{1,0:T(8,128)(2,1)}, bf16[640,512]{1,0:T(8,128)(2,1)S(1)}, u32[]{:S(2)}, u32[]{:S(2)}) collective-permute-start(bf16[640,512]{1,0:T(8,128)(2,1)} %get-tuple-element.48), channel_id=1, source_target_pairs={{0,8},{1,12},{2,10},{3,14},{4,0},{5,4},{6,2},{7,6},{8,9},{9,13},{1... | collective-permute-start | bytes 1966088 | tf_op jit(solution)/shard_map/ppermute | solution.py:503
  26.4 4.0 %collective-permute-start.6 = (bf16[640,512]{1,0:T(8,128)(2,1)}, bf16[640,512]{1,0:T(8,128)(2,1)}, u32[]{:S(2)}, u32[]{:S(2)}) collective-permute-start(bf16[640,512]{1,0:T(8,128)(2,1)} %get-tuple-element.49), channel_id=1, source_target_pairs={{0,12},{1,0},{2,14},{3,2},{4,4},{5,8},{6,6},{7,10},{8,13},{9,1},{1... | collective-permute-start | bytes 1966088 | tf_op jit(solution)/shard_map/ppermute | solution.py:503
  36.3 4.2 %all-to-all-start.1 = ((bf16[4,192,512]{2,1,0:T(8,128)(2,1)}), bf16[4,192,512]{2,1,0:T(8,128)(2,1)S(1)}, u32[]{:S(2)}, u32[]{:S(2)}) async-start(bf16[4,192,512]{2,1,0:T(8,128)(2,1)} %select_sessions.1), calls=%async_computation.1 | async-start | bytes 1572864 | tf_op jit(solution)/shard_map/all_to_all | solution.py:442
  40.6 13.7 %delta_prep.1 = (bf16[4,8,256,128]{3,2,1,0:T(8,128)(2,1)}, f32[4,8,128,128]{3,2,1,0:T(8,128)}, bf16[4,8,128,128]{3,2,1,0:T(8,128)(2,1)}, bf16[4,8,128,128]{3,2,1,0:T(8,128)(2,1)}, f32[4,8,128]{2,1,0:T(8,128)}) custom-call(bf16[4,512,128]{2,1,0:T(8,128)(2,1)} %q_ref.3, bf16[4,512,128]{2,1,0:T(8,128)(2,1)} %k_ref, bf16[4,512,256]{2,1,0:T(8,128)(2,1)} %v_ref.1, ...), custom_call_target="tpu_custom_call" | custom-call | flops 100000000 | bytes 300000 | tf_op jit(solution)/shard_map/delta_prep/pallas_call | solution.py:110
  54.2 7.1 %delta_scan.1 = (bf16[4,4,128,256]{3,2,1,0:T(8,128)(2,1)}, f32[4,2,128,128]{3,2,1,0:T(8,128)}) custom-call(s32[4]{0:T(128)} %and_select_fusion.2.src_ref, bf16[8,192,512]{2,1,0:T(8,128)(2,1)} %copy-done.1, bf16[4,8,256,128]{3,2,1,0:T(8,128)(2,1)} %get-tuple-element.52.wq_ref, f32[4,8,128,128]{3,2,1,0:T(8,128)} %get-tuple-element.53.u_ref, ...), custom_call_target="tpu_custom_call" | custom-call | flops 100000000 | bytes 300000 | tf_op jit(solution)/shard_map/delta_scan/pallas_call | solution.py:171
  63.3 6.0 %all-to-all-start.2 = ((bf16[4,4,192,256]{3,2,1,0:T(8,128)(2,1)}), bf16[4,4,192,256]{3,2,1,0:T(8,128)(2,1)S(1)}, u32[]{:S(2)}, u32[]{:S(2)}) async-start(bf16[4,4,192,256]{3,2,1,0:T(8,128)(2,1)} %pad_maximum_fusion), calls=%async_computation.2 | async-start | bytes 3145728 | tf_op jit(solution)/shard_map/all_to_all | solution.py:442
  71.2 2.9 %collective-permute-start.9 = (bf16[4,128,512]{2,1,0:T(8,128)(2,1)}, bf16[4,128,512]{2,1,0:T(8,128)(2,1)S(1)}, u32[]{:S(2)}, u32[]{:S(2)}) collective-permute-start(bf16[4,128,512]{2,1,0:T(8,128)(2,1)} %stack_weights.2.r0), channel_id=1, source_target_pairs={{0,96},{32,0},{64,32},{96,64},{1,97},{33,1},{65,33},{97,65},{2,98}... | collective-permute-start | bytes 1572872 | tf_op jit(solution)/shard_map/ppermute | solution.py:434
  75.8 3.2 %collective-permute-start.13 = (bf16[512,512]{1,0:T(8,128)(2,1)}, bf16[512,512]{1,0:T(8,128)(2,1)}, u32[]{:S(2)}, u32[]{:S(2)}) collective-permute-start(bf16[512,512]{1,0:T(8,128)(2,1)} %get-tuple-element.74.r0), channel_id=1, source_target_pairs={{0,3},{1,0},{2,1},{3,2},{4,7},{5,4},{6,5},{7,6},{8,11},{9,8},{10,9... | collective-permute-start | bytes 1572872 | tf_op jit(solution)/shard_map/ppermute | solution.py:434
  79.8 15.5 %collective-permute-done.9.r3 = bf16[4,128,512]{2,1,0:T(8,128)(2,1)S(1)} collective-permute-done((bf16[4,128,512]{2,1,0:T(8,128)(2,1)}, bf16[4,128,512]{2,1,0:T(8,128)(2,1)S(1)}, u32[]{:S(2)}, u32[]{:S(2)}) %collective-permute-start.9) | collective-permute-done | bytes 524320 | tf_op jit(solution)/shard_map/ppermute | solution.py:434
  99.7 3.6 %merge_weights.1.own_hbm = bf16[4,512,512]{2,1,0:T(8,128)(2,1)} custom-call(s32[1]{0:T(128)} %bitcast.9.sc_ref, bf16[4,128,512]{2,1,0:T(8,128)(2,1)} %stack_weights.2.r0, bf16[4,128,512]{2,1,0:T(8,128)(2,1)} %copy-done.11, bf16[4,128,512]{2,1,0:T(8,128)(2,1)} %copy-done.10, bf16[4,128,512]{2,1,0:T(8,128)(2,1)} %copy-done.9), custom_call_target="tpu_custom_call" | custom-call | flops 100000000 | bytes 300000 | tf_op jit(solution)/shard_map/merge_weights/pallas_call | solution.py:302
  103.4 8.4 %collective-permute-done.11.r1 = bf16[512,512]{1,0:T(8,128)(2,1)} collective-permute-done((bf16[512,512]{1,0:T(8,128)(2,1)}, bf16[512,512]{1,0:T(8,128)(2,1)}, u32[]{:S(2)}, u32[]{:S(2)}) %collective-permute-start.11) | collective-permute-done | bytes 524320 | tf_op jit(solution)/shard_map/ppermute | solution.py:434
  111.8 3.0 %stack_weights.3.own_ref = bf16[4,512,512]{2,1,0:T(8,128)(2,1)} custom-call(bf16[512,512]{1,0:T(8,128)(2,1)} %get-tuple-element.74.r0, bf16[512,512]{1,0:T(8,128)(2,1)} %collective-permute-done.11.r1, bf16[512,512]{1,0:T(8,128)(2,1)} %collective-permute-done.12.r2, bf16[512,512]{1,0:T(8,128)(2,1)} %collective-permute-done.13.r3), custom_call_target="tpu_custom_call" | custom-call | flops 100000000 | bytes 300000 | tf_op jit(solution)/shard_map/stack_weights/pallas_call | solution.py:279
  121.1 7.8 %attention_project.2 = (bf16[128,2048]{1,0:T(8,128)(2,1)}, bf16[128,2048]{1,0:T(8,128)(2,1)}) custom-call(s32[6]{0:T(128)} %stack.67.sc_ref, bf16[640,512]{1,0:T(8,128)(2,1)} %copy-done.2, bf16[640,512]{1,0:T(8,128)(2,1)} %copy-done.3, bf16[640,512]{1,0:T(8,128)(2,1)} %copy-done.4, bf16[640,512]{1,0:T(8,128)(2,1)} %collective-permute-done.6.r3.q3, ...), custom_call_target="tpu_custom_call" | custom-call | flops 100000000 | bytes 300000 | tf_op jit(solution)/shard_map/attention_project/pallas_call | solution.py:406
  128.9 3.8 %collective-permute-done.h1 = bf16[4,128,256]{2,1,0:T(8,128)(2,1)S(1)} collective-permute-done((bf16[4,128,256]{2,1,0:T(8,128)(2,1)S(1)}, bf16[4,128,256]{2,1,0:T(8,128)(2,1)S(1)}, u32[]{:S(2)}, u32[]{:S(2)}) %collective-permute-start) | collective-permute-done | bytes 262176 | tf_op jit(solution)/shard_map/ppermute | solution.py:434
  134.8 6.5 %delta_project.1 = (bf16[128,2048]{1,0:T(8,128)(2,1)}, bf16[128,2048]{1,0:T(8,128)(2,1)}, bf16[128,2048]{1,0:T(8,128)(2,1)}, bf16[128,2048]{1,0:T(8,128)(2,1)}) custom-call(s32[2]{0:T(128)} %pad_add_fusion.sc_ref, bf16[4,128,256]{2,1,0:T(8,128)(2,1)} %get-tuple-element.68.h0, bf16[4,128,256]{2,1,0:T(8,128)(2,1)} %copy-done.15, ...), custom_call_target="tpu_custom_call" | custom-call | flops 100000000 | bytes 300000 | tf_op jit(solution)/shard_map/delta_project/pallas_call | solution.py:223
  141.3 4.3 %collective-permute-start.15 = (bf16[128,2048]{1,0:T(8,128)(2,1)}, bf16[128,2048]{1,0:T(8,128)(2,1)S(1)}, u32[]{:S(2)}, u32[]{:S(2)}) collective-permute-start(bf16[128,2048]{1,0:T(8,128)(2,1)} %get-tuple-element.79), channel_id=1, source_target_pairs={{0,8},{4,12},{8,0},{12,4},{1,9},{5,13},{9,1},{13,5},{2,10},{6,14},... | collective-permute-start | bytes 1572872 | tf_op jit(solution)/shard_map/ppermute | solution.py:434
  145.6 3.2 %collective-permute-start.17 = (bf16[128,2048]{1,0:T(8,128)(2,1)}, bf16[128,2048]{1,0:T(8,128)(2,1)S(1)}, u32[]{:S(2)}, u32[]{:S(2)}) collective-permute-start(bf16[128,2048]{1,0:T(8,128)(2,1)} %get-tuple-element.81), channel_id=1, source_target_pairs={{0,12},{4,0},{8,4},{12,8},{1,13},{5,1},{9,5},{13,9},{2,14},{6,2},{... | collective-permute-start | bytes 1572872 | tf_op jit(solution)/shard_map/ppermute | solution.py:434
  151.6 8.0 %attention_project.3 = (bf16[128,2048]{1,0:T(8,128)(2,1)}, bf16[128,2048]{1,0:T(8,128)(2,1)}) custom-call(s32[6]{0:T(128)} %stack.73.sc_ref, bf16[640,512]{1,0:T(8,128)(2,1)} %copy-done.2, bf16[640,512]{1,0:T(8,128)(2,1)} %copy-done.3, bf16[640,512]{1,0:T(8,128)(2,1)} %copy-done.4, bf16[640,512]{1,0:T(8,128)(2,1)} %collective-permute-done.6.r3.q3, ...), custom_call_target="tpu_custom_call" | custom-call | flops 100000000 | bytes 300000 | tf_op jit(solution)/shard_map/attention_project/pallas_call | solution.py:406
  159.7 3.3 %collective-permute-start.20 = (bf16[128,2048]{1,0:T(8,128)(2,1)}, bf16[128,2048]{1,0:T(8,128)(2,1)S(1)}, u32[]{:S(2)}, u32[]{:S(2)}) collective-permute-start(bf16[128,2048]{1,0:T(8,128)(2,1)} %get-tuple-element.85), channel_id=1, source_target_pairs={{0,3},{1,0},{2,1},{3,2},{4,7},{5,4},{6,5},{7,6},{8,11},{9,8},{10,9... | collective-permute-start | bytes 1572872 | tf_op jit(solution)/shard_map/ppermute | solution.py:434
  163.0 6.2 %collective-permute-done.16 = bf16[128,2048]{1,0:T(8,128)(2,1)S(1)} collective-permute-done((bf16[128,2048]{1,0:T(8,128)(2,1)}, bf16[128,2048]{1,0:T(8,128)(2,1)S(1)}, u32[]{:S(2)}, u32[]{:S(2)}) %collective-permute-start.16) | collective-permute-done | bytes 524320 | tf_op jit(solution)/shard_map/ppermute | solution.py:434
  170.3 5.6 %collective-permute-done.19 = bf16[128,2048]{1,0:T(8,128)(2,1)S(1)} collective-permute-done((bf16[128,2048]{1,0:T(8,128)(2,1)}, bf16[128,2048]{1,0:T(8,128)(2,1)S(1)}, u32[]{:S(2)}, u32[]{:S(2)}) %collective-permute-start.19) | collective-permute-done | bytes 524320 | tf_op jit(solution)/shard_map/ppermute | solution.py:434
  (97 shorter events, 37.4 us)
Async XLA Ops:
  5.7 27.0 %all-to-all-start = ((bf16[8,192,512]{2,1,0:T(8,128)(2,1)}), bf16[8,192,512]{2,1,0:T(8,128)(2,1)S(1)}, u32[]{:S(2)}, u32[]{:S(2)}) async-start(bf16[8,192,512]{2,1,0:T(8,128)(2,1)} %broadcast_select_fusion), calls=%async_computation | async-start | bytes 3145728 | tf_op jit(solution)/shard_map/all_to_all | solution.py:442
  16.0 45.4 %collective-permute-start.3 = (bf16[640,512]{1,0:T(8,128)(2,1)}, bf16[640,512]{1,0:T(8,128)(2,1)S(1)}, u32[]{:S(2)}, u32[]{:S(2)}) collective-permute-start(bf16[640,512]{1,0:T(8,128)(2,1)} %get-tuple-element.46), channel_id=1, source_target_pairs={{0,0},{1,4},{2,2},{3,6},{4,8},{5,12},{6,10},{7,14},{8,1},{9,5},{10... | collective-permute-start | bytes 1966088 | tf_op jit(solution)/shard_map/ppermute | solution.py:503
  17.7 43.7 %collective-permute-start.4 = (bf16[640,512]{1,0:T(8,128)(2,1)}, bf16[640,512]{1,0:T(8,128)(2,1)S(1)}, u32[]{:S(2)}, u32[]{:S(2)}) collective-permute-start(bf16[640,512]{1,0:T(8,128)(2,1)} %get-tuple-element.47), channel_id=1, source_target_pairs={{0,4},{1,8},{2,6},{3,10},{4,12},{5,0},{6,14},{7,2},{8,5},{9,9},{10... | collective-permute-start | bytes 1966088 | tf_op jit(solution)/shard_map/ppermute | solution.py:503
  22.8 38.6 %collective-permute-start.5 = (bf16[640,512]{1,0:T(8,128)(2,1)}, bf16[640,512]{1,0:T(8,128)(2,1)S(1)}, u32[]{:S(2)}, u32[]{:S(2)}) collective-permute-start(bf16[640,512]{1,0:T(8,128)(2,1)} %get-tuple-element.48), channel_id=1, source_target_pairs={{0,8},{1,12},{2,10},{3,14},{4,0},{5,4},{6,2},{7,6},{8,9},{9,13},{1... | collective-permute-start | bytes 1966088 | tf_op jit(solution)/shard_map/ppermute | solution.py:503
  26.4 35.0 %collective-permute-start.6 = (bf16[640,512]{1,0:T(8,128)(2,1)}, bf16[640,512]{1,0:T(8,128)(2,1)}, u32[]{:S(2)}, u32[]{:S(2)}) collective-permute-start(bf16[640,512]{1,0:T(8,128)(2,1)} %get-tuple-element.49), channel_id=1, source_target_pairs={{0,12},{1,0},{2,14},{3,2},{4,4},{5,8},{6,6},{7,10},{8,13},{9,1},{1... | collective-permute-start | bytes 1966088 | tf_op jit(solution)/shard_map/ppermute | solution.py:503
  36.3 25.1 %all-to-all-start.1 = ((bf16[4,192,512]{2,1,0:T(8,128)(2,1)}), bf16[4,192,512]{2,1,0:T(8,128)(2,1)S(1)}, u32[]{:S(2)}, u32[]{:S(2)}) async-start(bf16[4,192,512]{2,1,0:T(8,128)(2,1)} %select_sessions.1), calls=%async_computation.1 | async-start | bytes 1572864 | tf_op jit(solution)/shard_map/all_to_all | solution.py:442
  63.3 35.7 %all-to-all-start.2 = ((bf16[4,4,192,256]{3,2,1,0:T(8,128)(2,1)}), bf16[4,4,192,256]{3,2,1,0:T(8,128)(2,1)S(1)}, u32[]{:S(2)}, u32[]{:S(2)}) async-start(bf16[4,4,192,256]{3,2,1,0:T(8,128)(2,1)} %pad_maximum_fusion), calls=%async_computation.2 | async-start | bytes 3145728 | tf_op jit(solution)/shard_map/all_to_all | solution.py:442
  71.2 24.2 %collective-permute-start.9 = (bf16[4,128,512]{2,1,0:T(8,128)(2,1)}, bf16[4,128,512]{2,1,0:T(8,128)(2,1)S(1)}, u32[]{:S(2)}, u32[]{:S(2)}) collective-permute-start(bf16[4,128,512]{2,1,0:T(8,128)(2,1)} %stack_weights.2.r0), channel_id=1, source_target_pairs={{0,96},{32,0},{64,32},{96,64},{1,97},{33,1},{65,33},{97,65},{2,98}... | collective-permute-start | bytes 1572872 | tf_op jit(solution)/shard_map/ppermute | solution.py:434
  74.0 23.1 %collective-permute-start.8 = (bf16[4,128,512]{2,1,0:T(8,128)(2,1)}, bf16[4,128,512]{2,1,0:T(8,128)(2,1)S(1)}, u32[]{:S(2)}, u32[]{:S(2)}) collective-permute-start(bf16[4,128,512]{2,1,0:T(8,128)(2,1)} %stack_weights.2.r0), channel_id=1, source_target_pairs={{0,64},{32,96},{64,0},{96,32},{1,65},{33,97},{65,1},{97,33},{2,66}... | collective-permute-start | bytes 1572872 | tf_op jit(solution)/shard_map/ppermute | solution.py:434
  74.9 24.1 %collective-permute-start.7 = (bf16[4,128,512]{2,1,0:T(8,128)(2,1)}, bf16[4,128,512]{2,1,0:T(8,128)(2,1)S(1)}, u32[]{:S(2)}, u32[]{:S(2)}) collective-permute-start(bf16[4,128,512]{2,1,0:T(8,128)(2,1)} %stack_weights.2.r0), channel_id=1, source_target_pairs={{0,32},{32,64},{64,96},{96,0},{1,33},{33,65},{65,97},{97,1},{2,34}... | collective-permute-start | bytes 1572872 | tf_op jit(solution)/shard_map/ppermute | solution.py:434
  75.8 27.7 %collective-permute-start.13 = (bf16[512,512]{1,0:T(8,128)(2,1)}, bf16[512,512]{1,0:T(8,128)(2,1)}, u32[]{:S(2)}, u32[]{:S(2)}) collective-permute-start(bf16[512,512]{1,0:T(8,128)(2,1)} %get-tuple-element.74.r0), channel_id=1, source_target_pairs={{0,3},{1,0},{2,1},{3,2},{4,7},{5,4},{6,5},{7,6},{8,11},{9,8},{10,9... | collective-permute-start | bytes 1572872 | tf_op jit(solution)/shard_map/ppermute | solution.py:434
  79.0 24.4 %collective-permute-start.12 = (bf16[512,512]{1,0:T(8,128)(2,1)}, bf16[512,512]{1,0:T(8,128)(2,1)}, u32[]{:S(2)}, u32[]{:S(2)}) collective-permute-start(bf16[512,512]{1,0:T(8,128)(2,1)} %get-tuple-element.74.r0), channel_id=1, source_target_pairs={{0,2},{1,3},{2,0},{3,1},{4,6},{5,7},{6,4},{7,5},{8,10},{9,11},{10,... | collective-permute-start | bytes 1572872 | tf_op jit(solution)/shard_map/ppermute | solution.py:434
  95.4 16.4 %collective-permute-start.11 = (bf16[512,512]{1,0:T(8,128)(2,1)}, bf16[512,512]{1,0:T(8,128)(2,1)}, u32[]{:S(2)}, u32[]{:S(2)}) collective-permute-start(bf16[512,512]{1,0:T(8,128)(2,1)} %get-tuple-element.74.r0), channel_id=1, source_target_pairs={{0,1},{1,2},{2,3},{3,0},{4,5},{5,6},{6,7},{7,4},{8,9},{9,10},{10,1... | collective-permute-start | bytes 1572872 | tf_op jit(solution)/shard_map/ppermute | solution.py:434
  103.3 17.7 %collective-permute-start.10 = (bf16[4,512,512]{2,1,0:T(8,128)(2,1)}, bf16[4,512,512]{2,1,0:T(8,128)(2,1)}, u32[]{:S(2)}, u32[]{:S(2)}) collective-permute-start(bf16[4,512,512]{2,1,0:T(8,128)(2,1)} %merge_weights.1.own_hbm), channel_id=1, source_target_pairs={{0,16},{16,0},{1,17},{17,1},{2,18},{18,2},{3,19},{19,3},{4,20},{20... | collective-permute-start | bytes 6291464 | tf_op jit(solution)/shard_map/ppermute | solution.py:506
  114.8 17.9 %collective-permute-start.14 = (bf16[4,512,512]{2,1,0:T(8,128)(2,1)}, bf16[4,512,512]{2,1,0:T(8,128)(2,1)S(1)}, u32[]{:S(2)}, u32[]{:S(2)}) collective-permute-start(bf16[4,512,512]{2,1,0:T(8,128)(2,1)} %stack_weights.3.own_ref), channel_id=1, source_target_pairs={{0,16},{16,0},{1,17},{17,1},{2,18},{18,2},{3,19},{19,3},{4,20},{20... | collective-permute-start | bytes 6291464 | tf_op jit(solution)/shard_map/ppermute | solution.py:506
  115.7 13.2 %collective-permute-start.2 = (bf16[4,128,256]{2,1,0:T(8,128)(2,1)}, bf16[4,128,256]{2,1,0:T(8,128)(2,1)S(1)}, u32[]{:S(2)}, u32[]{:S(2)}) collective-permute-start(bf16[4,128,256]{2,1,0:T(8,128)(2,1)} %get-tuple-element.87), channel_id=1, source_target_pairs={{0,3},{1,0},{2,1},{3,2},{4,7},{5,4},{6,5},{7,6},{8,11},{9,8},{10,9... | collective-permute-start | bytes 786440 | tf_op jit(solution)/shard_map/ppermute | solution.py:434
  116.9 12.0 %collective-permute-start.1 = (bf16[4,128,256]{2,1,0:T(8,128)(2,1)}, bf16[4,128,256]{2,1,0:T(8,128)(2,1)S(1)}, u32[]{:S(2)}, u32[]{:S(2)}) collective-permute-start(bf16[4,128,256]{2,1,0:T(8,128)(2,1)} %get-tuple-element.88), channel_id=1, source_target_pairs={{0,2},{1,3},{2,0},{3,1},{4,6},{5,7},{6,4},{7,5},{8,10},{9,11},{10,... | collective-permute-start | bytes 786440 | tf_op jit(solution)/shard_map/ppermute | solution.py:434
  118.4 14.3 %collective-permute-start = (bf16[4,128,256]{2,1,0:T(8,128)(2,1)S(1)}, bf16[4,128,256]{2,1,0:T(8,128)(2,1)S(1)}, u32[]{:S(2)}, u32[]{:S(2)}) collective-permute-start(bf16[4,128,256]{2,1,0:T(8,128)(2,1)S(1)} %get-tuple-element.89), channel_id=1, source_target_pairs={{0,1},{1,2},{2,3},{3,0},{4,5},{5,6},{6,7},{7,4},{8,9},{9,10},{10,1... | collective-permute-start | bytes 786440 | tf_op jit(solution)/shard_map/ppermute | solution.py:434
  141.3 18.4 %collective-permute-start.15 = (bf16[128,2048]{1,0:T(8,128)(2,1)}, bf16[128,2048]{1,0:T(8,128)(2,1)S(1)}, u32[]{:S(2)}, u32[]{:S(2)}) collective-permute-start(bf16[128,2048]{1,0:T(8,128)(2,1)} %get-tuple-element.79), channel_id=1, source_target_pairs={{0,8},{4,12},{8,0},{12,4},{1,9},{5,13},{9,1},{13,5},{2,10},{6,14},... | collective-permute-start | bytes 1572872 | tf_op jit(solution)/shard_map/ppermute | solution.py:434
  145.6 23.6 %collective-permute-start.16 = (bf16[128,2048]{1,0:T(8,128)(2,1)}, bf16[128,2048]{1,0:T(8,128)(2,1)S(1)}, u32[]{:S(2)}, u32[]{:S(2)}) collective-permute-start(bf16[128,2048]{1,0:T(8,128)(2,1)} %get-tuple-element.80), channel_id=1, source_target_pairs={{0,4},{4,8},{8,12},{12,0},{1,5},{5,9},{9,13},{13,1},{2,6},{6,10},{... | collective-permute-start | bytes 1572872 | tf_op jit(solution)/shard_map/ppermute | solution.py:434
  145.6 23.6 %collective-permute-start.17 = (bf16[128,2048]{1,0:T(8,128)(2,1)}, bf16[128,2048]{1,0:T(8,128)(2,1)S(1)}, u32[]{:S(2)}, u32[]{:S(2)}) collective-permute-start(bf16[128,2048]{1,0:T(8,128)(2,1)} %get-tuple-element.81), channel_id=1, source_target_pairs={{0,12},{4,0},{8,4},{12,8},{1,13},{5,1},{9,5},{13,9},{2,14},{6,2},{... | collective-permute-start | bytes 1572872 | tf_op jit(solution)/shard_map/ppermute | solution.py:434
  150.2 25.7 %collective-permute-start.18 = (bf16[128,2048]{1,0:T(8,128)(2,1)S(1)}, bf16[128,2048]{1,0:T(8,128)(2,1)S(1)}, u32[]{:S(2)}, u32[]{:S(2)}) collective-permute-start(bf16[128,2048]{1,0:T(8,128)(2,1)S(1)} %copy-done.17), channel_id=1, source_target_pairs={{0,2},{1,3},{2,0},{3,1},{4,6},{5,7},{6,4},{7,5},{8,10},{9,11},{10,... | collective-permute-start | bytes 1572872 | tf_op jit(solution)/shard_map/ppermute | solution.py:434
  151.6 24.3 %collective-permute-start.19 = (bf16[128,2048]{1,0:T(8,128)(2,1)}, bf16[128,2048]{1,0:T(8,128)(2,1)S(1)}, u32[]{:S(2)}, u32[]{:S(2)}) collective-permute-start(bf16[128,2048]{1,0:T(8,128)(2,1)} %get-tuple-element.84), channel_id=1, source_target_pairs={{0,1},{1,2},{2,3},{3,0},{4,5},{5,6},{6,7},{7,4},{8,9},{9,10},{10,1... | collective-permute-start | bytes 1572872 | tf_op jit(solution)/shard_map/ppermute | solution.py:434
  159.7 16.3 %collective-permute-start.20 = (bf16[128,2048]{1,0:T(8,128)(2,1)}, bf16[128,2048]{1,0:T(8,128)(2,1)S(1)}, u32[]{:S(2)}, u32[]{:S(2)}) collective-permute-start(bf16[128,2048]{1,0:T(8,128)(2,1)} %get-tuple-element.85), channel_id=1, source_target_pairs={{0,3},{1,0},{2,1},{3,2},{4,7},{5,4},{6,5},{7,6},{8,11},{9,8},{10,9... | collective-permute-start | bytes 1572872 | tf_op jit(solution)/shard_map/ppermute | solution.py:434
  (19 other events, 114.3 us)

commit v4 on v3

--- a/solution.py
+++ b/solution.py
@@ -527,11 +527,11 @@
 
     eighths = stack_rows(after(queries, leaving), CH, 4)
     eighths = [eighths] + [shift(eighths, "z", d) for d in (1, 2, 3)]
-    delta_own = stack_rows(after(delta_own, positions), 512, 0)
-    delta_other = swap_cores(delta_own)
     scalars = jnp.stack([x, core]).astype(jnp.int32)
     attn_own = merge_rows(z[None], after(eighths, positions))
     attn_other = swap_cores(attn_own)
+    delta_own = stack_rows(after(delta_own, attn_own), 512, 0)
+    delta_other = swap_cores(delta_own)
 
     def quarters(first, second, *others):
         asked = jnp.stack([x, y, length, (y + first) & 3, (y + second) & 3, core])

time: 179 us -> 186 us (1.039)
  waiting for transfers between devices: 41.3 us -> 50.5 us
    ppermute x15, waiting for transfers between devices: 41.3 us -> 50.5 us  [shift(): return lax.ppermute(array, axis, [(i, (i + by) % 4) for i in range(4)])]
    unnamed x39 -> x41, local copies, waits for them, and re-layouts: 4.21 us -> 4.2 us
  transfers between devices with their start and end apart: 24 -> 24, of which waited for: 6 -> 7; matrix products, arithmetic and copies ran while one was open for 5% -> 5% of each run, Pallas kernels for 29% -> 28%
where the time goes in v4:
time: 186 us; the launch traced here: 185 us
  Pallas kernels  58.3 us (31%)
  starting transfers between devices  54.3 us (29%)
  waiting for transfers between devices  50.5 us (27%)
  local copies, waits for them, and re-layouts  10.9 us (6%)
  other arithmetic  9.93 us (5%)
    ppermute x15, waiting for transfers between devices, shift(): return lax.ppermute(array, axis, [(i, (i + by) % 4) for i in range(4)])  50.5 us
    ppermute x15, starting transfers between devices, shift(): return lax.ppermute(array, axis, [(i, (i + by) % 4) for i in range(4)])  24.2 us
    pallas_call x2, Pallas kernels, attention(): pl.pallas_call(attention_kernel, grid_spec=pltpu.PrefetchScalarGridSpec(n...  15.8 us
    all_to_all x3, starting transfers between devices, all_to_all(): return lax.all_to_all(array, axis, split_axis=0, concat_axis=0, tiled=True)  15.5 us
    ppermute x4, starting transfers between devices, regrouped(): return lax.ppermute(array, ('x', 'y'), regroup(k))  14.5 us
    pallas_call x1, Pallas kernels, prep(): pl.pallas_call(prep_kernel, grid=(chunks,), in_specs=[spec_tok(CH), spec_...  13.7 us
    pallas_call x1, Pallas kernels, scan(): pl.pallas_call(scan_kernel, grid_spec=pltpu.PrefetchScalarGridSpec(num_sc...  7.13 us
    pallas_call x1, Pallas kernels, delta_project(): pl.pallas_call(delta_project_kernel, grid_spec=pltpu.PrefetchScalarGridSp...  6.52 us
  transfers between devices with their start and end apart: 24, of which 7 were waited for; matrix products, arithmetic and copies ran while one was open for 5% of the time, Pallas kernels for 28%

profile of v4, /device:TPU:0, one launch (start us, length us, event | category | flops | bytes accessed | tf_op | source)
XLA Modules:
  0.0 184.9 jit_solution(2545092470006937688)
XLA Ops:
  5.7 5.4 %all-to-all-start = ((bf16[8,192,512]{2,1,0:T(8,128)(2,1)}), bf16[8,192,512]{2,1,0:T(8,128)(2,1)S(1)}, u32[]{:S(2)}, u32[]{:S(2)}) async-start(bf16[8,192,512]{2,1,0:T(8,128)(2,1)} %broadcast_select_fusion), calls=%async_computation | async-start | bytes 3145728 | tf_op jit(solution)/shard_map/all_to_all | solution.py:442
  11.7 4.3 %pack_queries.1 = (bf16[640,512]{1,0:T(8,128)(2,1)}, bf16[640,512]{1,0:T(8,128)(2,1)}, bf16[640,512]{1,0:T(8,128)(2,1)}, bf16[640,512]{1,0:T(8,128)(2,1)}, bf16[512,512]{1,0:T(8,128)(2,1)}) custom-call(s32[3]{0:T(128)} %pad_add_fusion.1.sc_ref, bf16[4,512,256]{2,1,0:T(8,128)(2,1)} %q_ref.2, bf16[4,512,256]{2,1,0:T(8,128)(2,1)} %g_ref.2, ...), custom_call_target="tpu_custom_call" | custom-call | flops 100000000 | bytes 300000 | tf_op jit(solution)/shard_map/pack_queries/pallas_call | solution.py:251
  17.7 5.1 %collective-permute-start.4 = (bf16[640,512]{1,0:T(8,128)(2,1)}, bf16[640,512]{1,0:T(8,128)(2,1)S(1)}, u32[]{:S(2)}, u32[]{:S(2)}) collective-permute-start(bf16[640,512]{1,0:T(8,128)(2,1)} %get-tuple-element.47), channel_id=1, source_target_pairs={{0,4},{1,8},{2,6},{3,10},{4,12},{5,0},{6,14},{7,2},{8,5},{9,9},{10... | collective-permute-start | bytes 1966088 | tf_op jit(solution)/shard_map/ppermute | solution.py:503
  22.8 3.7 %collective-permute-start.5 = (bf16[640,512]{1,0:T(8,128)(2,1)}, bf16[640,512]{1,0:T(8,128)(2,1)S(1)}, u32[]{:S(2)}, u32[]{:S(2)}) collective-permute-start(bf16[640,512]{1,0:T(8,128)(2,1)} %get-tuple-element.48), channel_id=1, source_target_pairs={{0,8},{1,12},{2,10},{3,14},{4,0},{5,4},{6,2},{7,6},{8,9},{9,13},{1... | collective-permute-start | bytes 1966088 | tf_op jit(solution)/shard_map/ppermute | solution.py:503
  26.4 4.0 %collective-permute-start.6 = (bf16[640,512]{1,0:T(8,128)(2,1)}, bf16[640,512]{1,0:T(8,128)(2,1)}, u32[]{:S(2)}, u32[]{:S(2)}) collective-permute-start(bf16[640,512]{1,0:T(8,128)(2,1)} %get-tuple-element.49), channel_id=1, source_target_pairs={{0,12},{1,0},{2,14},{3,2},{4,4},{5,8},{6,6},{7,10},{8,13},{9,1},{1... | collective-permute-start | bytes 1966088 | tf_op jit(solution)/shard_map/ppermute | solution.py:503
  36.4 4.2 %all-to-all-start.1 = ((bf16[4,192,512]{2,1,0:T(8,128)(2,1)}), bf16[4,192,512]{2,1,0:T(8,128)(2,1)S(1)}, u32[]{:S(2)}, u32[]{:S(2)}) async-start(bf16[4,192,512]{2,1,0:T(8,128)(2,1)} %select_sessions.1), calls=%async_computation.1 | async-start | bytes 1572864 | tf_op jit(solution)/shard_map/all_to_all | solution.py:442
  40.6 13.7 %delta_prep.1 = (bf16[4,8,256,128]{3,2,1,0:T(8,128)(2,1)}, f32[4,8,128,128]{3,2,1,0:T(8,128)}, bf16[4,8,128,128]{3,2,1,0:T(8,128)(2,1)}, bf16[4,8,128,128]{3,2,1,0:T(8,128)(2,1)}, f32[4,8,128]{2,1,0:T(8,128)}) custom-call(bf16[4,512,128]{2,1,0:T(8,128)(2,1)} %q_ref.3, bf16[4,512,128]{2,1,0:T(8,128)(2,1)} %k_ref, bf16[4,512,256]{2,1,0:T(8,128)(2,1)} %v_ref.1, ...), custom_call_target="tpu_custom_call" | custom-call | flops 100000000 | bytes 300000 | tf_op jit(solution)/shard_map/delta_prep/pallas_call | solution.py:110
  54.2 7.1 %delta_scan.1 = (bf16[4,4,128,256]{3,2,1,0:T(8,128)(2,1)}, f32[4,2,128,128]{3,2,1,0:T(8,128)}) custom-call(s32[4]{0:T(128)} %and_select_fusion.2.src_ref, bf16[8,192,512]{2,1,0:T(8,128)(2,1)} %copy-done.1, bf16[4,8,256,128]{3,2,1,0:T(8,128)(2,1)} %get-tuple-element.52.wq_ref, f32[4,8,128,128]{3,2,1,0:T(8,128)} %get-tuple-element.53.u_ref, ...), custom_call_target="tpu_custom_call" | custom-call | flops 100000000 | bytes 300000 | tf_op jit(solution)/shard_map/delta_scan/pallas_call | solution.py:171
  63.3 6.0 %all-to-all-start.2 = ((bf16[4,4,192,256]{3,2,1,0:T(8,128)(2,1)}), bf16[4,4,192,256]{3,2,1,0:T(8,128)(2,1)S(1)}, u32[]{:S(2)}, u32[]{:S(2)}) async-start(bf16[4,4,192,256]{3,2,1,0:T(8,128)(2,1)} %pad_maximum_fusion), calls=%async_computation.2 | async-start | bytes 3145728 | tf_op jit(solution)/shard_map/all_to_all | solution.py:442
  71.2 2.9 %collective-permute-start.9 = (bf16[4,128,512]{2,1,0:T(8,128)(2,1)}, bf16[4,128,512]{2,1,0:T(8,128)(2,1)S(1)}, u32[]{:S(2)}, u32[]{:S(2)}) collective-permute-start(bf16[4,128,512]{2,1,0:T(8,128)(2,1)} %stack_weights.2.r0), channel_id=1, source_target_pairs={{0,96},{32,0},{64,32},{96,64},{1,97},{33,1},{65,33},{97,65},{2,98}... | collective-permute-start | bytes 1572872 | tf_op jit(solution)/shard_map/ppermute | solution.py:434
  75.8 3.2 %collective-permute-start.13 = (bf16[512,512]{1,0:T(8,128)(2,1)}, bf16[512,512]{1,0:T(8,128)(2,1)}, u32[]{:S(2)}, u32[]{:S(2)}) collective-permute-start(bf16[512,512]{1,0:T(8,128)(2,1)} %get-tuple-element.74.r0), channel_id=1, source_target_pairs={{0,3},{1,0},{2,1},{3,2},{4,7},{5,4},{6,5},{7,6},{8,11},{9,8},{10,9... | collective-permute-start | bytes 1572872 | tf_op jit(solution)/shard_map/ppermute | solution.py:434
  79.8 15.5 %collective-permute-done.9.r3 = bf16[4,128,512]{2,1,0:T(8,128)(2,1)S(1)} collective-permute-done((bf16[4,128,512]{2,1,0:T(8,128)(2,1)}, bf16[4,128,512]{2,1,0:T(8,128)(2,1)S(1)}, u32[]{:S(2)}, u32[]{:S(2)}) %collective-permute-start.9) | collective-permute-done | bytes 524320 | tf_op jit(solution)/shard_map/ppermute | solution.py:434
  99.7 3.6 %merge_weights.1.own_hbm = bf16[4,512,512]{2,1,0:T(8,128)(2,1)} custom-call(s32[1]{0:T(128)} %bitcast.9.sc_ref, bf16[4,128,512]{2,1,0:T(8,128)(2,1)} %stack_weights.2.r0, bf16[4,128,512]{2,1,0:T(8,128)(2,1)} %copy-done.11, bf16[4,128,512]{2,1,0:T(8,128)(2,1)} %copy-done.10, bf16[4,128,512]{2,1,0:T(8,128)(2,1)} %copy-done.9), custom_call_target="tpu_custom_call" | custom-call | flops 100000000 | bytes 300000 | tf_op jit(solution)/shard_map/merge_weights/pallas_call | solution.py:302
  103.4 8.4 %collective-permute-done.11.r1 = bf16[512,512]{1,0:T(8,128)(2,1)} collective-permute-done((bf16[512,512]{1,0:T(8,128)(2,1)}, bf16[512,512]{1,0:T(8,128)(2,1)}, u32[]{:S(2)}, u32[]{:S(2)}) %collective-permute-start.11) | collective-permute-done | bytes 524320 | tf_op jit(solution)/shard_map/ppermute | solution.py:434
  111.8 3.0 %stack_weights.3.own_ref = bf16[4,512,512]{2,1,0:T(8,128)(2,1)} custom-call(bf16[512,512]{1,0:T(8,128)(2,1)} %get-tuple-element.74.r0, bf16[512,512]{1,0:T(8,128)(2,1)} %collective-permute-done.11.r1, bf16[512,512]{1,0:T(8,128)(2,1)} %collective-permute-done.12.r2, bf16[512,512]{1,0:T(8,128)(2,1)} %collective-permute-done.13.r3), custom_call_target="tpu_custom_call" | custom-call | flops 100000000 | bytes 300000 | tf_op jit(solution)/shard_map/stack_weights/pallas_call | solution.py:279
  120.9 7.9 %attention_project.2 = (bf16[128,2048]{1,0:T(8,128)(2,1)}, bf16[128,2048]{1,0:T(8,128)(2,1)}) custom-call(s32[6]{0:T(128)} %stack.67.sc_ref, bf16[640,512]{1,0:T(8,128)(2,1)} %copy-done.2, bf16[640,512]{1,0:T(8,128)(2,1)} %copy-done.3, bf16[640,512]{1,0:T(8,128)(2,1)} %copy-done.4, bf16[640,512]{1,0:T(8,128)(2,1)} %collective-permute-done.6.r3.q3, ...), custom_call_target="tpu_custom_call" | custom-call | flops 100000000 | bytes 300000 | tf_op jit(solution)/shard_map/attention_project/pallas_call | solution.py:406
  128.8 3.9 %collective-permute-done.h1 = bf16[4,128,256]{2,1,0:T(8,128)(2,1)S(1)} collective-permute-done((bf16[4,128,256]{2,1,0:T(8,128)(2,1)S(1)}, bf16[4,128,256]{2,1,0:T(8,128)(2,1)S(1)}, u32[]{:S(2)}, u32[]{:S(2)}) %collective-permute-start) | collective-permute-done | bytes 262176 | tf_op jit(solution)/shard_map/ppermute | solution.py:434
  134.8 6.5 %delta_project.1 = (bf16[128,2048]{1,0:T(8,128)(2,1)}, bf16[128,2048]{1,0:T(8,128)(2,1)}, bf16[128,2048]{1,0:T(8,128)(2,1)}, bf16[128,2048]{1,0:T(8,128)(2,1)}) custom-call(s32[2]{0:T(128)} %pad_add_fusion.sc_ref, bf16[4,128,256]{2,1,0:T(8,128)(2,1)} %get-tuple-element.68.h0, bf16[4,128,256]{2,1,0:T(8,128)(2,1)} %copy-done.15, ...), custom_call_target="tpu_custom_call" | custom-call | flops 100000000 | bytes 300000 | tf_op jit(solution)/shard_map/delta_project/pallas_call | solution.py:223
  141.3 4.3 %collective-permute-start.15 = (bf16[128,2048]{1,0:T(8,128)(2,1)}, bf16[128,2048]{1,0:T(8,128)(2,1)S(1)}, u32[]{:S(2)}, u32[]{:S(2)}) collective-permute-start(bf16[128,2048]{1,0:T(8,128)(2,1)} %get-tuple-element.79), channel_id=1, source_target_pairs={{0,8},{4,12},{8,0},{12,4},{1,9},{5,13},{9,1},{13,5},{2,10},{6,14},... | collective-permute-start | bytes 1572872 | tf_op jit(solution)/shard_map/ppermute | solution.py:434
  145.6 3.2 %collective-permute-start.17 = (bf16[128,2048]{1,0:T(8,128)(2,1)}, bf16[128,2048]{1,0:T(8,128)(2,1)S(1)}, u32[]{:S(2)}, u32[]{:S(2)}) collective-permute-start(bf16[128,2048]{1,0:T(8,128)(2,1)} %get-tuple-element.81), channel_id=1, source_target_pairs={{0,12},{4,0},{8,4},{12,8},{1,13},{5,1},{9,5},{13,9},{2,14},{6,2},{... | collective-permute-start | bytes 1572872 | tf_op jit(solution)/shard_map/ppermute | solution.py:434
  150.1 8.0 %attention_project.3 = (bf16[128,2048]{1,0:T(8,128)(2,1)}, bf16[128,2048]{1,0:T(8,128)(2,1)}) custom-call(s32[6]{0:T(128)} %stack.73.sc_ref, bf16[640,512]{1,0:T(8,128)(2,1)} %copy-done.2, bf16[640,512]{1,0:T(8,128)(2,1)} %copy-done.3, bf16[640,512]{1,0:T(8,128)(2,1)} %copy-done.4, bf16[640,512]{1,0:T(8,128)(2,1)} %collective-permute-done.6.r3.q3, ...), custom_call_target="tpu_custom_call" | custom-call | flops 100000000 | bytes 300000 | tf_op jit(solution)/shard_map/attention_project/pallas_call | solution.py:406
  161.7 7.4 %collective-permute-done.16 = bf16[128,2048]{1,0:T(8,128)(2,1)S(1)} collective-permute-done((bf16[128,2048]{1,0:T(8,128)(2,1)}, bf16[128,2048]{1,0:T(8,128)(2,1)S(1)}, u32[]{:S(2)}, u32[]{:S(2)}) %collective-permute-start.16) | collective-permute-done | bytes 524320 | tf_op jit(solution)/shard_map/ppermute | solution.py:434
  170.3 3.0 %collective-permute-done.20 = bf16[128,2048]{1,0:T(8,128)(2,1)S(1)} collective-permute-done((bf16[128,2048]{1,0:T(8,128)(2,1)}, bf16[128,2048]{1,0:T(8,128)(2,1)S(1)}, u32[]{:S(2)}, u32[]{:S(2)}) %collective-permute-start.20) | collective-permute-done | bytes 524320 | tf_op jit(solution)/shard_map/ppermute | solution.py:434
  173.3 10.5 %collective-permute-done.19 = bf16[128,2048]{1,0:T(8,128)(2,1)S(1)} collective-permute-done((bf16[128,2048]{1,0:T(8,128)(2,1)S(1)}, bf16[128,2048]{1,0:T(8,128)(2,1)S(1)}, u32[]{:S(2)}, u32[]{:S(2)}) %collective-permute-start.19) | collective-permute-done | bytes 524320 | tf_op jit(solution)/shard_map/ppermute | solution.py:434
  (99 shorter events, 39.4 us)
Async XLA Ops:
  5.7 27.1 %all-to-all-start = ((bf16[8,192,512]{2,1,0:T(8,128)(2,1)}), bf16[8,192,512]{2,1,0:T(8,128)(2,1)S(1)}, u32[]{:S(2)}, u32[]{:S(2)}) async-start(bf16[8,192,512]{2,1,0:T(8,128)(2,1)} %broadcast_select_fusion), calls=%async_computation | async-start | bytes 3145728 | tf_op jit(solution)/shard_map/all_to_all | solution.py:442
  16.0 45.4 %collective-permute-start.3 = (bf16[640,512]{1,0:T(8,128)(2,1)}, bf16[640,512]{1,0:T(8,128)(2,1)S(1)}, u32[]{:S(2)}, u32[]{:S(2)}) collective-permute-start(bf16[640,512]{1,0:T(8,128)(2,1)} %get-tuple-element.46), channel_id=1, source_target_pairs={{0,0},{1,4},{2,2},{3,6},{4,8},{5,12},{6,10},{7,14},{8,1},{9,5},{10... | collective-permute-start | bytes 1966088 | tf_op jit(solution)/shard_map/ppermute | solution.py:503
  17.7 43.7 %collective-permute-start.4 = (bf16[640,512]{1,0:T(8,128)(2,1)}, bf16[640,512]{1,0:T(8,128)(2,1)S(1)}, u32[]{:S(2)}, u32[]{:S(2)}) collective-permute-start(bf16[640,512]{1,0:T(8,128)(2,1)} %get-tuple-element.47), channel_id=1, source_target_pairs={{0,4},{1,8},{2,6},{3,10},{4,12},{5,0},{6,14},{7,2},{8,5},{9,9},{10... | collective-permute-start | bytes 1966088 | tf_op jit(solution)/shard_map/ppermute | solution.py:503
  22.8 38.6 %collective-permute-start.5 = (bf16[640,512]{1,0:T(8,128)(2,1)}, bf16[640,512]{1,0:T(8,128)(2,1)S(1)}, u32[]{:S(2)}, u32[]{:S(2)}) collective-permute-start(bf16[640,512]{1,0:T(8,128)(2,1)} %get-tuple-element.48), channel_id=1, source_target_pairs={{0,8},{1,12},{2,10},{3,14},{4,0},{5,4},{6,2},{7,6},{8,9},{9,13},{1... | collective-permute-start | bytes 1966088 | tf_op jit(solution)/shard_map/ppermute | solution.py:503
  26.4 35.0 %collective-permute-start.6 = (bf16[640,512]{1,0:T(8,128)(2,1)}, bf16[640,512]{1,0:T(8,128)(2,1)}, u32[]{:S(2)}, u32[]{:S(2)}) collective-permute-start(bf16[640,512]{1,0:T(8,128)(2,1)} %get-tuple-element.49), channel_id=1, source_target_pairs={{0,12},{1,0},{2,14},{3,2},{4,4},{5,8},{6,6},{7,10},{8,13},{9,1},{1... | collective-permute-start | bytes 1966088 | tf_op jit(solution)/shard_map/ppermute | solution.py:503
  36.4 25.0 %all-to-all-start.1 = ((bf16[4,192,512]{2,1,0:T(8,128)(2,1)}), bf16[4,192,512]{2,1,0:T(8,128)(2,1)S(1)}, u32[]{:S(2)}, u32[]{:S(2)}) async-start(bf16[4,192,512]{2,1,0:T(8,128)(2,1)} %select_sessions.1), calls=%async_computation.1 | async-start | bytes 1572864 | tf_op jit(solution)/shard_map/all_to_all | solution.py:442
  63.3 35.7 %all-to-all-start.2 = ((bf16[4,4,192,256]{3,2,1,0:T(8,128)(2,1)}), bf16[4,4,192,256]{3,2,1,0:T(8,128)(2,1)S(1)}, u32[]{:S(2)}, u32[]{:S(2)}) async-start(bf16[4,4,192,256]{3,2,1,0:T(8,128)(2,1)} %pad_maximum_fusion), calls=%async_computation.2 | async-start | bytes 3145728 | tf_op jit(solution)/shard_map/all_to_all | solution.py:442
  71.2 24.2 %collective-permute-start.9 = (bf16[4,128,512]{2,1,0:T(8,128)(2,1)}, bf16[4,128,512]{2,1,0:T(8,128)(2,1)S(1)}, u32[]{:S(2)}, u32[]{:S(2)}) collective-permute-start(bf16[4,128,512]{2,1,0:T(8,128)(2,1)} %stack_weights.2.r0), channel_id=1, source_target_pairs={{0,96},{32,0},{64,32},{96,64},{1,97},{33,1},{65,33},{97,65},{2,98}... | collective-permute-start | bytes 1572872 | tf_op jit(solution)/shard_map/ppermute | solution.py:434
  74.0 23.1 %collective-permute-start.8 = (bf16[4,128,512]{2,1,0:T(8,128)(2,1)}, bf16[4,128,512]{2,1,0:T(8,128)(2,1)S(1)}, u32[]{:S(2)}, u32[]{:S(2)}) collective-permute-start(bf16[4,128,512]{2,1,0:T(8,128)(2,1)} %stack_weights.2.r0), channel_id=1, source_target_pairs={{0,64},{32,96},{64,0},{96,32},{1,65},{33,97},{65,1},{97,33},{2,66}... | collective-permute-start | bytes 1572872 | tf_op jit(solution)/shard_map/ppermute | solution.py:434
  74.9 24.0 %collective-permute-start.7 = (bf16[4,128,512]{2,1,0:T(8,128)(2,1)}, bf16[4,128,512]{2,1,0:T(8,128)(2,1)S(1)}, u32[]{:S(2)}, u32[]{:S(2)}) collective-permute-start(bf16[4,128,512]{2,1,0:T(8,128)(2,1)} %stack_weights.2.r0), channel_id=1, source_target_pairs={{0,32},{32,64},{64,96},{96,0},{1,33},{33,65},{65,97},{97,1},{2,34}... | collective-permute-start | bytes 1572872 | tf_op jit(solution)/shard_map/ppermute | solution.py:434
  75.8 27.7 %collective-permute-start.13 = (bf16[512,512]{1,0:T(8,128)(2,1)}, bf16[512,512]{1,0:T(8,128)(2,1)}, u32[]{:S(2)}, u32[]{:S(2)}) collective-permute-start(bf16[512,512]{1,0:T(8,128)(2,1)} %get-tuple-element.74.r0), channel_id=1, source_target_pairs={{0,3},{1,0},{2,1},{3,2},{4,7},{5,4},{6,5},{7,6},{8,11},{9,8},{10,9... | collective-permute-start | bytes 1572872 | tf_op jit(solution)/shard_map/ppermute | solution.py:434
  79.0 24.4 %collective-permute-start.12 = (bf16[512,512]{1,0:T(8,128)(2,1)}, bf16[512,512]{1,0:T(8,128)(2,1)}, u32[]{:S(2)}, u32[]{:S(2)}) collective-permute-start(bf16[512,512]{1,0:T(8,128)(2,1)} %get-tuple-element.74.r0), channel_id=1, source_target_pairs={{0,2},{1,3},{2,0},{3,1},{4,6},{5,7},{6,4},{7,5},{8,10},{9,11},{10,... | collective-permute-start | bytes 1572872 | tf_op jit(solution)/shard_map/ppermute | solution.py:434
  95.4 16.4 %collective-permute-start.11 = (bf16[512,512]{1,0:T(8,128)(2,1)}, bf16[512,512]{1,0:T(8,128)(2,1)}, u32[]{:S(2)}, u32[]{:S(2)}) collective-permute-start(bf16[512,512]{1,0:T(8,128)(2,1)} %get-tuple-element.74.r0), channel_id=1, source_target_pairs={{0,1},{1,2},{2,3},{3,0},{4,5},{5,6},{6,7},{7,4},{8,9},{9,10},{10,1... | collective-permute-start | bytes 1572872 | tf_op jit(solution)/shard_map/ppermute | solution.py:434
  103.3 17.6 %collective-permute-start.10 = (bf16[4,512,512]{2,1,0:T(8,128)(2,1)}, bf16[4,512,512]{2,1,0:T(8,128)(2,1)}, u32[]{:S(2)}, u32[]{:S(2)}) collective-permute-start(bf16[4,512,512]{2,1,0:T(8,128)(2,1)} %merge_weights.1.own_hbm), channel_id=1, source_target_pairs={{0,16},{16,0},{1,17},{17,1},{2,18},{18,2},{3,19},{19,3},{4,20},{20... | collective-permute-start | bytes 6291464 | tf_op jit(solution)/shard_map/ppermute | solution.py:506
  114.8 17.9 %collective-permute-start.14 = (bf16[4,512,512]{2,1,0:T(8,128)(2,1)}, bf16[4,512,512]{2,1,0:T(8,128)(2,1)S(1)}, u32[]{:S(2)}, u32[]{:S(2)}) collective-permute-start(bf16[4,512,512]{2,1,0:T(8,128)(2,1)} %stack_weights.3.own_ref), channel_id=1, source_target_pairs={{0,16},{16,0},{1,17},{17,1},{2,18},{18,2},{3,19},{19,3},{4,20},{20... | collective-permute-start | bytes 6291464 | tf_op jit(solution)/shard_map/ppermute | solution.py:506
  115.7 13.1 %collective-permute-start.2 = (bf16[4,128,256]{2,1,0:T(8,128)(2,1)}, bf16[4,128,256]{2,1,0:T(8,128)(2,1)S(1)}, u32[]{:S(2)}, u32[]{:S(2)}) collective-permute-start(bf16[4,128,256]{2,1,0:T(8,128)(2,1)} %get-tuple-element.87), channel_id=1, source_target_pairs={{0,3},{1,0},{2,1},{3,2},{4,7},{5,4},{6,5},{7,6},{8,11},{9,8},{10,9... | collective-permute-start | bytes 786440 | tf_op jit(solution)/shard_map/ppermute | solution.py:434
  116.9 11.9 %collective-permute-start.1 = (bf16[4,128,256]{2,1,0:T(8,128)(2,1)}, bf16[4,128,256]{2,1,0:T(8,128)(2,1)S(1)}, u32[]{:S(2)}, u32[]{:S(2)}) collective-permute-start(bf16[4,128,256]{2,1,0:T(8,128)(2,1)} %get-tuple-element.88), channel_id=1, source_target_pairs={{0,2},{1,3},{2,0},{3,1},{4,6},{5,7},{6,4},{7,5},{8,10},{9,11},{10,... | collective-permute-start | bytes 786440 | tf_op jit(solution)/shard_map/ppermute | solution.py:434
  118.4 14.3 %collective-permute-start = (bf16[4,128,256]{2,1,0:T(8,128)(2,1)S(1)}, bf16[4,128,256]{2,1,0:T(8,128)(2,1)S(1)}, u32[]{:S(2)}, u32[]{:S(2)}) collective-permute-start(bf16[4,128,256]{2,1,0:T(8,128)(2,1)S(1)} %get-tuple-element.89), channel_id=1, source_target_pairs={{0,1},{1,2},{2,3},{3,0},{4,5},{5,6},{6,7},{7,4},{8,9},{9,10},{10,1... | collective-permute-start | bytes 786440 | tf_op jit(solution)/shard_map/ppermute | solution.py:434
  141.3 19.0 %collective-permute-start.15 = (bf16[128,2048]{1,0:T(8,128)(2,1)}, bf16[128,2048]{1,0:T(8,128)(2,1)S(1)}, u32[]{:S(2)}, u32[]{:S(2)}) collective-permute-start(bf16[128,2048]{1,0:T(8,128)(2,1)} %get-tuple-element.79), channel_id=1, source_target_pairs={{0,8},{4,12},{8,0},{12,4},{1,9},{5,13},{9,1},{13,5},{2,10},{6,14},... | collective-permute-start | bytes 1572872 | tf_op jit(solution)/shard_map/ppermute | solution.py:434
  145.6 23.5 %collective-permute-start.16 = (bf16[128,2048]{1,0:T(8,128)(2,1)}, bf16[128,2048]{1,0:T(8,128)(2,1)S(1)}, u32[]{:S(2)}, u32[]{:S(2)}) collective-permute-start(bf16[128,2048]{1,0:T(8,128)(2,1)} %get-tuple-element.80), channel_id=1, source_target_pairs={{0,4},{4,8},{8,12},{12,0},{1,5},{5,9},{9,13},{13,1},{2,6},{6,10},{... | collective-permute-start | bytes 1572872 | tf_op jit(solution)/shard_map/ppermute | solution.py:434
  145.6 23.5 %collective-permute-start.17 = (bf16[128,2048]{1,0:T(8,128)(2,1)}, bf16[128,2048]{1,0:T(8,128)(2,1)S(1)}, u32[]{:S(2)}, u32[]{:S(2)}) collective-permute-start(bf16[128,2048]{1,0:T(8,128)(2,1)} %get-tuple-element.81), channel_id=1, source_target_pairs={{0,12},{4,0},{8,4},{12,8},{1,13},{5,1},{9,5},{13,9},{2,14},{6,2},{... | collective-permute-start | bytes 1572872 | tf_op jit(solution)/shard_map/ppermute | solution.py:434
  158.1 15.1 %collective-permute-start.20 = (bf16[128,2048]{1,0:T(8,128)(2,1)}, bf16[128,2048]{1,0:T(8,128)(2,1)S(1)}, u32[]{:S(2)}, u32[]{:S(2)}) collective-permute-start(bf16[128,2048]{1,0:T(8,128)(2,1)} %get-tuple-element.85), channel_id=1, source_target_pairs={{0,3},{1,0},{2,1},{3,2},{4,7},{5,4},{6,5},{7,6},{8,11},{9,8},{10,9... | collective-permute-start | bytes 1572872 | tf_op jit(solution)/shard_map/ppermute | solution.py:434
  158.8 24.9 %collective-permute-start.19 = (bf16[128,2048]{1,0:T(8,128)(2,1)S(1)}, bf16[128,2048]{1,0:T(8,128)(2,1)S(1)}, u32[]{:S(2)}, u32[]{:S(2)}) collective-permute-start(bf16[128,2048]{1,0:T(8,128)(2,1)S(1)} %copy-done.18), channel_id=1, source_target_pairs={{0,1},{1,2},{2,3},{3,0},{4,5},{5,6},{6,7},{7,4},{8,9},{9,10},{10,1... | collective-permute-start | bytes 1572872 | tf_op jit(solution)/shard_map/ppermute | solution.py:434
  160.2 23.5 %collective-permute-start.18 = (bf16[128,2048]{1,0:T(8,128)(2,1)S(1)}, bf16[128,2048]{1,0:T(8,128)(2,1)S(1)}, u32[]{:S(2)}, u32[]{:S(2)}) collective-permute-start(bf16[128,2048]{1,0:T(8,128)(2,1)S(1)} %copy-done.17), channel_id=1, source_target_pairs={{0,2},{1,3},{2,0},{3,1},{4,6},{5,7},{6,4},{7,5},{8,10},{9,11},{10,... | collective-permute-start | bytes 1572872 | tf_op jit(solution)/shard_map/ppermute | solution.py:434
  (20 other events, 126.7 us)
